TPU v7x, 32 devices: a whole 2x2x4 slice. The times are simulated.
32 devices in a mesh: dp: 4 (over z), seq: 2 (over core), heads: 4 (over y, x).
Axes of the slice: x: 2, y: 2, z: 4, core: 2. Of those that a mesh axis runs over, the one named last changes fastest.
Arguments:
- inputs: bfloat16 [2, 4, 1024, 1024], P(None, 'dp', ('seq', 'heads')), may hold values from -6 to 6
- w_qkv: bfloat16 [3, 1024, 1024], P(None, ('dp', 'seq'), 'heads'), may hold values from -0.1875 to 0.1875
- b_qv: bfloat16 [2, 16, 64], P(None, 'heads', ('dp', 'seq')), may hold values from -3 to 3
- w_out: bfloat16 [1024, 1024], P('heads', ('dp', 'seq')), may hold values from -3 to 3
- w_up: bfloat16 [1024, 4096], P(('dp', 'seq'), 'heads'), may hold values from -0.1875 to 0.1875
- b_up: bfloat16 [64, 64], P('heads', ('dp', 'seq')), may hold values from -3 to 3
- w_down: bfloat16 [4096, 1024], P('heads', ('dp', 'seq')), may hold values from -0.09375 to 0.09375
- ln_gains: bfloat16 [2, 1024], P(None, ('dp', 'seq')), may hold values from 0.5 to 1.5
- ln_shifts: bfloat16 [4, 1024], P(None, ('dp', 'seq')), may hold values from -2 to 2
- cotangent: bfloat16 [2, 4, 1024, 1024], P(None, 'dp', ('seq', 'heads')), may hold values from -6 to 6
Outputs:
- output: bfloat16 [2, 4, 1024, 1024], P(None, 'dp', ('seq', 'heads'))
- grad_inputs: bfloat16 [2, 4, 1024, 1024], P(None, 'dp', ('seq', 'heads'))
- grad_qkv: float32 [3, 1024, 1024], P(None, ('dp', 'seq'), 'heads')
- grad_bqv: float32 [2, 16, 64], P(None, 'heads', ('dp', 'seq'))
- grad_out: float32 [1024, 1024], P('heads', ('dp', 'seq'))
- grad_up: float32 [1024, 4096], P(('dp', 'seq'), 'heads')
- grad_bup: float32 [64, 64], P('heads', ('dp', 'seq'))
- grad_down: float32 [4096, 1024], P('heads', ('dp', 'seq'))
- grad_gains: float32 [2, 1024], P(None, ('dp', 'seq'))
- grad_shifts: float32 [4, 1024], P(None, ('dp', 'seq'))
All inputs are finite; a program needn't handle non-finite values.
Results may differ from a plain program's by a relative error of at most 0.02.
Values may be sent and summed in bfloat16 or wider, within the bound.
A program may use at most 64 MiB of HBM per device.

v0:
```python
import jax
import jax.numpy as jnp
from jax import lax
from jax.sharding import PartitionSpec as P

EPSILON = 1e-05


def norm_rows(value_in, gain, shift):
    centred = value_in - jnp.mean(value_in, -1, keepdims=True)
    spread = jnp.mean(centred * centred, -1, keepdims=True)
    return centred * lax.rsqrt(spread + EPSILON) * gain + shift


def gelu_exact(value_in):
    return jax.nn.gelu(value_in, approximate=False)


def attend(queries, key_rows, value_rows, heads_here, head_size):
    total_rows = queries.shape[0]
    block_rows = min(512, total_rows)
    blocks = total_rows // block_rows
    query_blocks = queries.reshape(blocks, block_rows, heads_here, head_size)
    key_heads = key_rows.reshape(-1, heads_here, head_size)
    value_heads = value_rows.reshape(-1, heads_here, head_size)

    def one_block(query_block):
        scores = (
            jnp.einsum("qhd,khd->hqk", query_block, key_heads, preferred_element_type=jnp.float32)
            * 0.125
        )
        largest = jnp.max(scores, -1, keepdims=True)
        weights = jnp.exp(scores - largest)
        totals = jnp.sum(weights, -1, keepdims=True)
        attn_probs = (weights / totals).astype(jnp.bfloat16)
        mixed_rows = jnp.einsum(
            "hqk,khd->qhd", attn_probs, value_heads, preferred_element_type=jnp.float32
        )
        return (mixed_rows.reshape(block_rows, -1), (largest + jnp.log(totals))[..., 0])

    mixed_rows, log_total = lax.map(one_block, query_blocks)
    return (mixed_rows.reshape(total_rows, -1), log_total)


def attend_back(queries, key_rows, value_rows, d_mixed, log_total, heads_here, head_size):
    blocks = log_total.shape[0]
    block_rows = log_total.shape[2]
    key_heads = key_rows.reshape(-1, heads_here, head_size)
    value_heads = value_rows.reshape(-1, heads_here, head_size)
    query_blocks = queries.reshape(blocks, block_rows, heads_here, head_size)
    grad_blocks = d_mixed.reshape(blocks, block_rows, heads_here, head_size)

    def one_block(running, pieces):
        d_key_sum, d_value_sum = running
        query_block, grad_block, log_block = pieces
        scores = (
            jnp.einsum("qhd,khd->hqk", query_block, key_heads, preferred_element_type=jnp.float32)
            * 0.125
        )
        attn_probs = jnp.exp(scores - log_block[..., None])
        d_probs = jnp.einsum(
            "qhd,khd->hqk", grad_block, value_heads, preferred_element_type=jnp.float32
        )
        centre = jnp.sum(attn_probs * d_probs, -1, keepdims=True)
        d_scores = (attn_probs * (d_probs - centre)).astype(jnp.bfloat16)
        d_query = (
            jnp.einsum("hqk,khd->qhd", d_scores, key_heads, preferred_element_type=jnp.float32)
            * 0.125
        )
        d_key_sum = (
            d_key_sum
            + jnp.einsum("hqk,qhd->khd", d_scores, query_block, preferred_element_type=jnp.float32)
            * 0.125
        )
        d_value_sum = d_value_sum + jnp.einsum(
            "hqk,qhd->khd",
            attn_probs.astype(jnp.bfloat16),
            grad_block,
            preferred_element_type=jnp.float32,
        )
        return ((d_key_sum, d_value_sum), d_query.reshape(block_rows, -1))

    zero_rows = jnp.zeros(key_heads.shape, jnp.float32)
    (d_key_sum, d_value_sum), d_query = lax.scan(
        one_block, (zero_rows, zero_rows), (query_blocks, grad_blocks, log_total)
    )
    key_count = key_rows.shape[0]
    return (
        d_query.reshape(queries.shape[0], -1),
        d_key_sum.reshape(key_count, -1),
        d_value_sum.reshape(key_count, -1),
    )


def forward_pass(x_rows, weights_now):
    w_qkv, b_qv, w_out, w_up, b_up, w_down, ln_gains, ln_shifts = weights_now
    gain_rows = ln_gains.astype(jnp.float32)
    shift_rows = ln_shifts.astype(jnp.float32)
    heads_here = b_qv.shape[1]
    head_size = b_qv.shape[2]
    gathered = lax.all_gather(x_rows, "heads", axis=0, tiled=True)
    projected = jnp.einsum("rd,tdc->trc", gathered, w_qkv, preferred_element_type=jnp.float32)
    query_bias = b_qv[0].reshape(-1).astype(jnp.float32)
    bias_rows = jnp.stack(
        [query_bias, jnp.zeros_like(query_bias), b_qv[1].reshape(-1).astype(jnp.float32)]
    )
    qkv_rows = (projected + bias_rows[:, None, :]).astype(jnp.bfloat16)
    queries = qkv_rows[0]
    key_rows, value_rows = (
        lax.all_gather(qkv_rows[1], "seq", axis=0, tiled=True),
        lax.all_gather(qkv_rows[2], "seq", axis=0, tiled=True),
    )
    attended, log_total = attend(queries, key_rows, value_rows, heads_here, head_size)
    attended_low = attended.astype(jnp.bfloat16)
    first_rows = (
        x_rows.astype(jnp.float32)
        + lax.psum_scatter(
            jnp.dot(attended_low, w_out, preferred_element_type=jnp.float32).astype(jnp.bfloat16),
            "heads",
            scatter_dimension=0,
            tiled=True,
        ).astype(jnp.float32)
        + shift_rows[0]
    )
    normed_rows = norm_rows(first_rows, gain_rows[0], shift_rows[1]).astype(jnp.bfloat16)
    normed_all = lax.all_gather(normed_rows, "heads", axis=0, tiled=True)
    hidden_pre = jnp.dot(normed_all, w_up, preferred_element_type=jnp.float32) + b_up.reshape(
        -1
    ).astype(jnp.float32)
    hidden = gelu_exact(hidden_pre).astype(jnp.bfloat16)
    second_rows = (
        normed_rows.astype(jnp.float32)
        + lax.psum_scatter(
            jnp.dot(hidden, w_down, preferred_element_type=jnp.float32).astype(jnp.bfloat16),
            "heads",
            scatter_dimension=0,
            tiled=True,
        ).astype(jnp.float32)
        + shift_rows[2]
    )
    result_rows = norm_rows(second_rows, gain_rows[1], shift_rows[3]).astype(jnp.bfloat16)
    stored = (
        gathered,
        queries,
        key_rows,
        value_rows,
        log_total,
        attended_low,
        first_rows,
        normed_all,
        hidden_pre,
        hidden,
        second_rows,
    )
    return (result_rows, stored)


def backward_pass(grad_rows, weights_now, stored):
    w_qkv, b_qv, w_out, w_up, b_up, w_down, ln_gains, ln_shifts = weights_now
    (
        gathered,
        queries,
        key_rows,
        value_rows,
        log_total,
        attended_low,
        first_rows,
        normed_all,
        hidden_pre,
        hidden,
        second_rows,
    ) = stored
    gain_rows = ln_gains.astype(jnp.float32)
    shift_rows = ln_shifts.astype(jnp.float32)
    heads_here = b_qv.shape[1]
    head_size = b_qv.shape[2]
    unused_two, pull_two = jax.vjp(norm_rows, second_rows, gain_rows[1], shift_rows[3])
    d_second, d_gain_two, d_shift_two = pull_two(grad_rows.astype(jnp.float32))
    d_mlp = d_second.astype(jnp.bfloat16)
    d_mlp_all = lax.all_gather(d_mlp, "heads", axis=0, tiled=True)
    g_down = jnp.einsum("rf,rd->fd", hidden, d_mlp_all, preferred_element_type=jnp.float32)
    d_hidden = jnp.einsum("rd,fd->rf", d_mlp_all, w_down, preferred_element_type=jnp.float32)
    unused_gelu, pull_gelu = jax.vjp(gelu_exact, hidden_pre)
    d_pre = pull_gelu(d_hidden)[0].astype(jnp.bfloat16)
    g_up = jnp.einsum("rd,rf->df", normed_all, d_pre, preferred_element_type=jnp.float32)
    g_bup = jnp.sum(d_pre.astype(jnp.float32), 0).reshape(b_up.shape)
    d_normed = (
        lax.psum_scatter(
            jnp.einsum("rf,df->rd", d_pre, w_up, preferred_element_type=jnp.float32).astype(
                jnp.bfloat16
            ),
            "heads",
            scatter_dimension=0,
            tiled=True,
        ).astype(jnp.float32)
        + d_second
    )
    unused_one, pull_one = jax.vjp(norm_rows, first_rows, gain_rows[0], shift_rows[1])
    d_first, d_gain_one, d_shift_one = pull_one(d_normed)
    d_attn = d_first.astype(jnp.bfloat16)
    d_attn_all = lax.all_gather(d_attn, "heads", axis=0, tiled=True)
    g_out = jnp.einsum("rc,rd->cd", attended_low, d_attn_all, preferred_element_type=jnp.float32)
    d_mixed = jnp.einsum("rd,cd->rc", d_attn_all, w_out, preferred_element_type=jnp.float32).astype(
        jnp.bfloat16
    )
    d_query, d_keys, d_values = attend_back(
        queries, key_rows, value_rows, d_mixed, log_total, heads_here, head_size
    )
    d_keys, d_values = (
        lax.psum_scatter(
            d_keys.astype(jnp.bfloat16), "seq", scatter_dimension=0, tiled=True
        ).astype(jnp.float32),
        lax.psum_scatter(
            d_values.astype(jnp.bfloat16), "seq", scatter_dimension=0, tiled=True
        ).astype(jnp.float32),
    )
    d_qkv = jnp.stack([d_query, d_keys, d_values]).astype(jnp.bfloat16)
    g_qkv = jnp.einsum("rd,trc->tdc", gathered, d_qkv, preferred_element_type=jnp.float32)
    bias_sums = jnp.sum(d_qkv.astype(jnp.float32), 1)
    g_bqv = jnp.stack([bias_sums[0], bias_sums[2]]).reshape(2, heads_here, head_size)
    d_inputs = (
        lax.psum_scatter(
            jnp.einsum("trc,tdc->rd", d_qkv, w_qkv, preferred_element_type=jnp.float32).astype(
                jnp.bfloat16
            ),
            "heads",
            scatter_dimension=0,
            tiled=True,
        ).astype(jnp.float32)
        + d_first
    )
    g_gain = jnp.stack([d_gain_one, d_gain_two])
    g_shift = jnp.stack(
        [
            jnp.sum(d_attn.astype(jnp.float32), 0),
            d_shift_one,
            jnp.sum(d_mlp.astype(jnp.float32), 0),
            d_shift_two,
        ]
    )
    return (
        d_inputs.astype(jnp.bfloat16),
        (g_qkv, g_bqv, g_out, g_up, g_bup, g_down, g_gain, g_shift),
    )


def local(inputs, w_qkv, b_qv, w_out, w_up, b_up, w_down, ln_gains, ln_shifts, cotangent):

    def fetch_weights():
        return (
            lax.all_gather(w_qkv, ("dp", "seq"), axis=1, tiled=True),
            lax.all_gather(b_qv, ("dp", "seq"), axis=2, tiled=True),
            lax.all_gather(w_out, ("dp", "seq"), axis=1, tiled=True),
            lax.all_gather(w_up, ("dp", "seq"), axis=0, tiled=True),
            lax.all_gather(b_up, ("dp", "seq"), axis=1, tiled=True),
            lax.all_gather(w_down, ("dp", "seq"), axis=1, tiled=True),
            lax.all_gather(ln_gains, ("dp", "seq"), axis=1, tiled=True),
            lax.all_gather(ln_shifts, ("dp", "seq"), axis=1, tiled=True),
        )

    micro_count = inputs.shape[0]
    result_list = []
    grad_list = []
    grads_total = None
    for micro_index in range(micro_count):
        weights_now = fetch_weights()
        result_rows, stored = forward_pass(inputs[micro_index, 0], weights_now)
        result_list.append(result_rows)
        weights_now = fetch_weights()
        d_inputs, grads_now = backward_pass(cotangent[micro_index, 0], weights_now, stored)
        grad_list.append(d_inputs)
        if grads_total is None:
            grads_total = grads_now
        else:
            grads_total = jax.tree.map(jnp.add, grads_total, grads_now)
    summed = (
        lax.psum_scatter(
            grads_total[0].astype(jnp.bfloat16), ("dp", "seq"), scatter_dimension=1, tiled=True
        ).astype(jnp.float32),
        lax.psum_scatter(
            grads_total[1].astype(jnp.bfloat16), ("dp", "seq"), scatter_dimension=2, tiled=True
        ).astype(jnp.float32),
        lax.psum_scatter(
            grads_total[2].astype(jnp.bfloat16), ("dp", "seq"), scatter_dimension=1, tiled=True
        ).astype(jnp.float32),
        lax.psum_scatter(
            grads_total[3].astype(jnp.bfloat16), ("dp", "seq"), scatter_dimension=0, tiled=True
        ).astype(jnp.float32),
        lax.psum_scatter(
            grads_total[4].astype(jnp.bfloat16), ("dp", "seq"), scatter_dimension=1, tiled=True
        ).astype(jnp.float32),
        lax.psum_scatter(
            grads_total[5].astype(jnp.bfloat16), ("dp", "seq"), scatter_dimension=1, tiled=True
        ).astype(jnp.float32),
        lax.psum_scatter(
            grads_total[6].astype(jnp.bfloat16), ("dp", "seq"), scatter_dimension=1, tiled=True
        ).astype(jnp.float32),
        lax.psum_scatter(
            grads_total[7].astype(jnp.bfloat16), ("dp", "seq"), scatter_dimension=1, tiled=True
        ).astype(jnp.float32),
    )
    gain_total, shift_total = lax.psum((summed[6], summed[7]), "heads")
    return (
        jnp.stack(result_list)[:, None],
        jnp.stack(grad_list)[:, None],
        summed[0],
        summed[1],
        summed[2],
        summed[3],
        summed[4],
        summed[5],
        gain_total,
        shift_total,
    )


def solution(mesh):
    in_specs = (
        P(None, "dp", ("seq", "heads"), None),
        P(None, ("dp", "seq"), "heads"),
        P(None, "heads", ("dp", "seq")),
        P("heads", ("dp", "seq")),
        P(("dp", "seq"), "heads"),
        P("heads", ("dp", "seq")),
        P("heads", ("dp", "seq")),
        P(None, ("dp", "seq")),
        P(None, ("dp", "seq")),
        P(None, "dp", ("seq", "heads"), None),
    )
    out_specs = (
        P(None, "dp", ("seq", "heads"), None),
        P(None, "dp", ("seq", "heads"), None),
        P(None, ("dp", "seq"), "heads"),
        P(None, "heads", ("dp", "seq")),
        P("heads", ("dp", "seq")),
        P(("dp", "seq"), "heads"),
        P("heads", ("dp", "seq")),
        P("heads", ("dp", "seq")),
        P(None, ("dp", "seq")),
        P(None, ("dp", "seq")),
    )
    return jax.shard_map(local, mesh=mesh, in_specs=in_specs, out_specs=out_specs, check_vma=False)
```

profile of v0, /device:TPU:0, one launch (start us, length us, event | category | flops | bytes accessed | tf_op | source)
XLA Modules:
  0.0 864.2 jit_solution(2526216868471862521)
XLA Ops:
  11.8 15.7 %all_gather.80 = bf16[2,4,64]{1,0,2:T(2,128)(2,1)S(1)} all-gather(bf16[2,4,8]{1,0,2:T(2,128)(2,1)S(1)} %copy.106), channel_id=1, replica_groups=mesh['dp'=4,'seq'=2,'heads'=4] {'dp','seq'}, dimensions={2}, use_global_device_ids=true | all-gather | bytes 1152 | tf_op jit(solution)/shard_map/all_gather | solution.py:252
  28.1 13.7 %all_gather.83 = bf16[256,1024]{1,0:T(8,128)(2,1)S(1)} all-gather(bf16[256,128]{1,0:T(8,128)(2,1)S(1)} %copy-done.50), channel_id=1, replica_groups=mesh['dp'=4,'seq'=2,'heads'=4] {'dp','seq'}, dimensions={1}, use_global_device_ids=true | all-gather | bytes 589824 | tf_op jit(solution)/shard_map/all_gather | solution.py:253
  41.8 27.4 %all-gather.18.cloned.1.call-done = bf16[3,1024,256]{1,2,0:T(8,128)(2,1)} async-done(((bf16[3,128,256]{1,2,0:T(8,128)(2,1)}), bf16[3,1024,256]{1,2,0:T(8,128)(2,1)}) %all-gather.18.cloned.1.call-update) | async-done | bytes 1572880 | tf_op jit(solution)/shard_map/all_gather | solution.py:251
  76.3 21.1 %all-gather.38.cloned.1.call-done = bf16[1,1,512,1024]{3,2,1,0:T(8,128)(2,1)} async-done(((bf16[1,1,128,1024]{3,2,1,0:T(8,128)(2,1)}), bf16[1,1,512,1024]{3,2,1,0:T(8,128)(2,1)}) %all-gather.38.cloned.1.call-update) | async-done | bytes 1048592 | tf_op jit(solution)/shard_map/all_gather | solution.py:101
  120.8 11.7 %all_gather.85 = bf16[2,1024]{1,0:T(2,128)(2,1)S(1)} all-gather(bf16[2,128]{1,0:T(2,128)(2,1)S(1)} %copy-done.54), channel_id=1, replica_groups=mesh['dp'=4,'seq'=2,'heads'=4] {'dp','seq'}, dimensions={1}, use_global_device_ids=true | all-gather | bytes 4608 | tf_op jit(solution)/shard_map/all_gather | solution.py:257
  132.5 9.1 %all_gather.84 = bf16[4,1024]{1,0:T(4,128)(2,1)S(1)} all-gather(bf16[4,128]{1,0:T(4,128)(2,1)S(1)} %copy-done.53), channel_id=1, replica_groups=mesh['dp'=4,'seq'=2,'heads'=4] {'dp','seq'}, dimensions={1}, use_global_device_ids=true | all-gather | bytes 9216 | tf_op jit(solution)/shard_map/all_gather | solution.py:258
  142.9 26.6 %reduce-scatter.35.cloned.1.call-done = bf16[128,1024]{1,0:T(8,128)(2,1)} async-done(((bf16[512,1024]{1,0:T(8,128)(2,1)}), bf16[128,1024]{1,0:T(8,128)(2,1)}) %reduce-scatter.35.cloned.1.call-update) | async-done | bytes 262160 | tf_op jit(solution)/shard_map/reduce_scatter | solution.py:117
  175.6 12.9 %all_gather.88 = bf16[16,64]{0,1:T(8,128)(2,1)S(1)} all-gather(bf16[16,8]{0,1:T(8,128)(2,1)S(1)} %copy-done.52), channel_id=1, replica_groups=mesh['dp'=4,'seq'=2,'heads'=4] {'dp','seq'}, dimensions={1}, use_global_device_ids=true | all-gather | bytes 2304 | tf_op jit(solution)/shard_map/all_gather | solution.py:255
  188.6 11.6 %all-gather.22.cloned.1.call-done = bf16[1024,1024]{1,0:T(8,128)(2,1)} async-done(((bf16[128,1024]{1,0:T(8,128)(2,1)}), bf16[1024,1024]{1,0:T(8,128)(2,1)}) %all-gather.22.cloned.1.call-update) | async-done | bytes 2097168 | tf_op jit(solution)/shard_map/all_gather | solution.py:254
  200.1 28.5 %all-gather.20.cloned.1.call-done = bf16[512,1024]{1,0:T(8,128)(2,1)} async-done(((bf16[128,1024]{1,0:T(8,128)(2,1)}), bf16[512,1024]{1,0:T(8,128)(2,1)}) %all-gather.20.cloned.1.call-update) | async-done | bytes 1048592 | tf_op jit(solution)/shard_map/all_gather | solution.py:126
  228.7 4.5 fusion.100
  233.2 24.6 %all-gather.26.cloned.1.call-done = bf16[512,1024]{1,0:T(8,128)(2,1)} async-done(((bf16[128,1024]{1,0:T(8,128)(2,1)}), bf16[512,1024]{1,0:T(8,128)(2,1)}) %all-gather.26.cloned.1.call-update) | async-done | bytes 1048592 | tf_op jit(solution)/shard_map/all_gather | solution.py:126
  257.7 13.1 %multiply_convert_fusion.2 = (bf16[512,1024]{1,0:T(8,128)(2,1)}, f32[512,1024]{1,0:T(8,128)}, bf16[512,1024]{1,0:T(8,128)(2,1)S(1)}, f32[512,1024]{1,0:T(8,128)}, f32[512,1024]{1,0:T(8,128)}) fusion(f32[1024]{0:T(1024)S(1)} %reshape.294, f32[512,1024]{1,0:T(8,128)} %fusion.100, bf16[512,1024]{1,0:T(8,128)(2,1)} %all-gather.26.cloned.1.call-done, ...), kind=kOutput, calls=%fused_computation.37 | convolution fusion | flops 1142947840 | bytes 13635584 | tf_op jit(solution)/shard_map/dot_general | solution.py:127
  270.8 19.4 %all-gather.24.cloned.1.call-done = bf16[1024,1024]{1,0:T(8,128)(2,1)} async-done(((bf16[1024,128]{1,0:T(8,128)(2,1)}), bf16[1024,1024]{1,0:T(8,128)(2,1)}) %all-gather.24.cloned.1.call-update) | async-done | bytes 2097168 | tf_op jit(solution)/shard_map/all_gather | solution.py:256
  290.2 3.8 convolution_convert_fusion.4
  294.1 4.3 convolution_convert_fusion.2
  298.5 22.5 %reduce-scatter.33.cloned.1.call-done = bf16[128,1024]{1,0:T(8,128)(2,1)} async-done(((bf16[512,1024]{1,0:T(8,128)(2,1)}), bf16[128,1024]{1,0:T(8,128)(2,1)}) %reduce-scatter.33.cloned.1.call-update) | async-done | bytes 262160 | tf_op jit(solution)/shard_map/reduce_scatter | solution.py:133
  322.2 29.7 %reduce-scatter.37.cloned.1.call-done = bf16[128,1024]{1,0:T(8,128)(2,1)} async-done(((bf16[512,1024]{1,0:T(8,128)(2,1)}), bf16[128,1024]{1,0:T(8,128)(2,1)}) %reduce-scatter.37.cloned.1.call-update) | async-done | bytes 262160 | tf_op jit(solution)/shard_map/reduce_scatter | solution.py:133
  359.4 25.6 %all-gather.28.cloned.1.call-done = bf16[512,1024]{1,0:T(8,128)(2,1)} async-done(((bf16[128,1024]{1,0:T(8,128)(2,1)}), bf16[512,1024]{1,0:T(8,128)(2,1)}) %all-gather.28.cloned.1.call-update) | async-done | bytes 1048592 | tf_op jit(solution)/shard_map/all_gather | solution.py:180
  385.1 4.6 fusion.101
  389.6 24.5 %all-gather.32.cloned.1.call-done = bf16[512,1024]{1,0:T(8,128)(2,1)} async-done(((bf16[128,1024]{1,0:T(8,128)(2,1)}), bf16[512,1024]{1,0:T(8,128)(2,1)}) %all-gather.32.cloned.1.call-update) | async-done | bytes 1048592 | tf_op jit(solution)/shard_map/all_gather | solution.py:180
  414.1 9.0 %convert_reduce_fusion = (f32[1024]{0:T(1024)S(1)}, bf16[512,1024]{1,0:T(8,128)(2,1)}, f32[1024]{0:T(1024)S(1)}, bf16[512,1024]{1,0:T(8,128)(2,1)S(1)}) fusion(f32[512,1024]{1,0:T(8,128)} %get-tuple-element.206, f32[512,1024]{1,0:T(8,128)} %get-tuple-element.246, f32[1024]{0:T(1024)S(1)} %reshape.294, f32[512,1024]{1,0:T(8,128)} %fusion.101, ...), kind=kOutput, calls=%fused_computation.33 | convolution fusion | flops 1091565568 | bytes 15740928 | tf_op jit(solution)/shard_map/rd,fd->rf/dot_general | solution.py:182
  426.6 4.2 convolution_convert_fusion
  430.8 23.5 %reduce-scatter.39.cloned.1.call-done = bf16[128,1024]{1,0:T(8,128)(2,1)} async-done(((bf16[512,1024]{1,0:T(8,128)(2,1)}), bf16[128,1024]{1,0:T(8,128)(2,1)}) %reduce-scatter.39.cloned.1.call-update) | async-done | bytes 262160 | tf_op jit(solution)/shard_map/reduce_scatter | solution.py:188
  454.4 30.8 %reduce-scatter.47.cloned.1.call-done = bf16[128,1024]{1,0:T(8,128)(2,1)} async-done(((bf16[512,1024]{1,0:T(8,128)(2,1)}), bf16[128,1024]{1,0:T(8,128)(2,1)}) %reduce-scatter.47.cloned.1.call-update) | async-done | bytes 262160 | tf_op jit(solution)/shard_map/reduce_scatter | solution.py:188
  490.2 25.8 %all-gather.34.cloned.1.call-done = bf16[512,1024]{1,0:T(8,128)(2,1)} async-done(((bf16[128,1024]{1,0:T(8,128)(2,1)}), bf16[512,1024]{1,0:T(8,128)(2,1)}) %all-gather.34.cloned.1.call-update) | async-done | bytes 1048592 | tf_op jit(solution)/shard_map/all_gather | solution.py:201
  517.7 5.1 fusion.35
  523.8 6.8 multiply_reduce_fusion
  530.8 7.1 multiply_convert_fusion
  541.0 3.4 all-gather.30.cloned.1.call-done
  546.1 5.1 fusion.32
  552.1 6.8 multiply_reduce_fusion.1
  559.0 6.9 multiply_convert_fusion.1
  569.3 4.5 fusion.104
  575.7 4.2 add_convert_fusion
  593.8 3.7 fusion.39
  597.7 3.1 bitcast_convert_fusion
  600.9 3.6 fusion.38
  604.7 3.6 bitcast_convert_fusion.1
  624.4 30.1 %reduce-scatter.65.cloned.1.call-done = bf16[128,4]{1,0:T(8,128)(2,1)} async-done(((bf16[1024,4]{1,0:T(8,128)(2,1)}), bf16[128,4]{1,0:T(8,128)(2,1)}) %reduce-scatter.65.cloned.1.call-update) | async-done | bytes 1040
  655.3 10.4 %all-reduce.2 = (f32[2,128]{1,0:T(2,128)}, f32[4,128]{1,0:T(4,128)}) all-reduce(bf16[2,128]{1,0:T(2,128)(2,1)S(1)} %copy.139, bf16[4,128]{1,0:T(4,128)(2,1)S(1)} %copy.141), channel_id=1, replica_groups=mesh['dp'=4,'seq'=2,'heads'=4] {'heads'}, use_global_device_ids=true, to_apply=%region_49.50 | all-reduce | flops 768 | bytes 4608 | tf_op jit(solution)/shard_map/psum | solution.py:302
  665.7 24.9 %reduce-scatter.61.cloned.1.call-done = bf16[128,1024]{1,0:T(8,128)(2,1)} async-done(((bf16[1024,1024]{1,0:T(8,128)(2,1)}), bf16[128,1024]{1,0:T(8,128)(2,1)}) %reduce-scatter.61.cloned.1.call-update) | async-done | bytes 262160
  692.6 34.6 %reduce-scatter.55.cloned.1.call-done = bf16[128,1024]{1,0:T(8,128)(2,1)} async-done(((bf16[1024,1024]{1,0:T(8,128)(2,1)}), bf16[128,1024]{1,0:T(8,128)(2,1)}) %reduce-scatter.55.cloned.1.call-update) | async-done | bytes 262160 | tf_op jit(solution)/shard_map/reduce_scatter | solution.py:286
  729.0 30.0 %reduce-scatter.59.cloned.1.call-done = bf16[128,256]{1,0:T(8,128)(2,1)} async-done(((bf16[1024,256]{1,0:T(8,128)(2,1)}), bf16[128,256]{1,0:T(8,128)(2,1)}) %reduce-scatter.59.cloned.1.call-update) | async-done | bytes 65552
  761.0 13.9 %all-reduce.3 = (bf16[2,4,64]{2,1,0:T(4,128)(2,1)S(1)}, bf16[16,64]{1,0:T(8,128)(2,1)S(1)}) all-reduce(bf16[2,4,64]{2,1,0:T(4,128)(2,1)S(1)} %convert_element_type.428, bf16[16,64]{1,0:T(8,128)(2,1)S(1)} %convert_element_type.437), channel_id=21, replica_groups=mesh['dp'=4,'seq'=2,'heads'=4] {'dp','seq'}, use_global_device_ids=true, to_apply=%region_37.38.clone | all-reduce | flops 1536 | bytes 6144
  776.3 11.5 %reduce-scatter.53.cloned.1.call-done = bf16[128,1024]{1,0:T(8,128)(2,1)} async-done(((bf16[512,1024]{1,0:T(8,128)(2,1)}), bf16[128,1024]{1,0:T(8,128)(2,1)}) %reduce-scatter.53.cloned.1.call-update) | async-done | bytes 262160 | tf_op jit(solution)/shard_map/reduce_scatter | solution.py:222
  788.9 29.6 %reduce-scatter.45.cloned.1.call-done = bf16[128,1024]{1,0:T(8,128)(2,1)} async-done(((bf16[512,1024]{1,0:T(8,128)(2,1)}), bf16[128,1024]{1,0:T(8,128)(2,1)}) %reduce-scatter.45.cloned.1.call-update) | async-done | bytes 262160 | tf_op jit(solution)/shard_map/reduce_scatter | solution.py:222
  820.4 34.7 %reduce-scatter.57.cloned.1.call-done = bf16[128,768]{1,0:T(8,128)(2,1)} async-done(((bf16[1024,768]{1,0:T(8,128)(2,1)}), bf16[128,768]{1,0:T(8,128)(2,1)}) %reduce-scatter.57.cloned.1.call-update) | async-done | bytes 196624
  (295 shorter events, 116.5 us)
Async XLA Ops:
  7.2 20.9 %copy-start.50 = (bf16[256,128]{1,0:T(8,128)(2,1)S(1)}, bf16[256,128]{1,0:T(8,128)(2,1)}, u32[]{:S(2)}) copy-start(bf16[256,128]{1,0:T(8,128)(2,1)} %param.13) | copy-start | bytes 196612
  7.2 34.6 %all-gather.36.cloned.1.call-start = ((), (), s32[]{:S(2)}) async-start(), calls=%async_computation.40 | async-start | bytes 1310720 | tf_op jit(solution)/shard_map/all_gather | solution.py:101
  9.1 60.0 %all-gather.18.cloned.1.call-start = ((), (), s32[]{:S(2)}) async-start(), calls=%async_computation.18 | async-start | bytes 1769472 | tf_op jit(solution)/shard_map/all_gather | solution.py:251
  10.9 86.5 %all-gather.38.cloned.1.call-start = ((), (), s32[]{:S(2)}) async-start(), calls=%async_computation.41 | async-start | bytes 1310720 | tf_op jit(solution)/shard_map/all_gather | solution.py:101
  11.7 130.0 %reduce-scatter.31.cloned.1.call-start = ((), (), s32[]{:S(2)}) async-start(), calls=%async_computation.19 | async-start | bytes 1310720 | tf_op jit(solution)/shard_map/reduce_scatter | solution.py:117
  71.9 30.4 %copy-start.20 = (bf16[1,512,256]{1,2,0:T(8,128)(2,1)}, bf16[1,512,256]{1,2,0:T(8,128)(2,1)S(1)}, u32[]{:S(2)}) copy-start(bf16[1,512,256]{1,2,0:T(8,128)(2,1)S(1)} %get-tuple-element.213) | copy-start | bytes 786436
  74.1 28.2 %copy-start.13 = (bf16[1,1024,256]{1,2,0:T(8,128)(2,1)}, bf16[1,1024,256]{1,2,0:T(8,128)(2,1)S(1)}, u32[]{:S(2)}) copy-start(bf16[1,1024,256]{1,2,0:T(8,128)(2,1)S(1)} %all-gather.2) | copy-start | bytes 1572868
  76.3 29.3 %copy-start.24 = (bf16[1,1024,256]{1,2,0:T(8,128)(2,1)}, bf16[1,1024,256]{1,2,0:T(8,128)(2,1)S(1)}, u32[]{:S(2)}) copy-start(bf16[1,1024,256]{1,2,0:T(8,128)(2,1)S(1)} %all-gather.1) | copy-start | bytes 1572868
  110.8 58.6 %reduce-scatter.35.cloned.1.call-start = ((), (), s32[]{:S(2)}) async-start(), calls=%async_computation.24 | async-start | bytes 1310720 | tf_op jit(solution)/shard_map/reduce_scatter | solution.py:117
  118.7 52.1 %copy-start.39 = (bf16[4,64,512]{2,1,0:T(8,128)(2,1)}, bf16[4,64,512]{2,1,0:T(8,128)(2,1)S(1)}, u32[]{:S(2)}) copy-start(bf16[4,64,512]{2,1,0:T(8,128)(2,1)S(1)} %fusion.40) | copy-start | bytes 786436
  118.7 23.0 %copy-start.4 = (bf16[2,1,128,1024]{3,2,1,0:T(8,128)(2,1)S(1)}, bf16[2,1,128,1024]{3,2,1,0:T(8,128)(2,1)}, u32[]{:S(2)}) copy-start(bf16[2,1,128,1024]{3,2,1,0:T(8,128)(2,1)} %param.10) | copy-start | bytes 1572868
  120.2 80.0 %all-gather.22.cloned.1.call-start = ((), (), s32[]{:S(2)}) async-start(), calls=%async_computation.21 | async-start | bytes 2359296 | tf_op jit(solution)/shard_map/all_gather | solution.py:254
  120.8 107.9 %all-gather.20.cloned.1.call-start = ((), (), s32[]{:S(2)}) async-start(), calls=%async_computation.20 | async-start | bytes 1310720 | tf_op jit(solution)/shard_map/all_gather | solution.py:126
  141.7 30.3 %copy-start.7 = (bf16[128,1024]{1,0:T(8,128)(2,1)S(1)}, bf16[128,1024]{1,0:T(8,128)(2,1)}, u32[]{:S(2)}) copy-start(bf16[128,1024]{1,0:T(8,128)(2,1)} %reduce-scatter.31.cloned.1.call-done) | copy-start | bytes 786436
  142.9 32.7 %copy-start.52 = (bf16[16,8]{0,1:T(8,128)(2,1)S(1)}, bf16[16,8]{0,1:T(8,128)(2,1)}, u32[]{:S(2)}) copy-start(bf16[16,8]{0,1:T(8,128)(2,1)} %param.15) | copy-start | bytes 772
  174.0 83.7 %all-gather.26.cloned.1.call-start = ((), (), s32[]{:S(2)}) async-start(), calls=%async_computation.25 | async-start | bytes 1310720 | tf_op jit(solution)/shard_map/all_gather | solution.py:126
  174.8 115.4 %all-gather.24.cloned.1.call-start = ((), (), s32[]{:S(2)}) async-start(), calls=%async_computation.22 | async-start | bytes 2359296 | tf_op jit(solution)/shard_map/all_gather | solution.py:256
  175.5 145.5 %reduce-scatter.33.cloned.1.call-start = ((), (), s32[]{:S(2)}) async-start(), calls=%async_computation.23 | async-start | bytes 1310720 | tf_op jit(solution)/shard_map/reduce_scatter | solution.py:133
  270.8 23.2 %copy-start.29 = (bf16[512,1024]{1,0:T(8,128)(2,1)}, bf16[512,1024]{1,0:T(8,128)(2,1)S(1)}, u32[]{:S(2)}) copy-start(bf16[512,1024]{1,0:T(8,128)(2,1)S(1)} %get-tuple-element.240) | copy-start | bytes 3145732
  294.1 57.9 %reduce-scatter.37.cloned.1.call-start = ((), (), s32[]{:S(2)}) async-start(), calls=%async_computation.26 | async-start | bytes 1310720 | tf_op jit(solution)/shard_map/reduce_scatter | solution.py:133
  294.1 26.9 %copy-start.6 = (bf16[128,1024]{1,0:T(8,128)(2,1)S(1)}, bf16[128,1024]{1,0:T(8,128)(2,1)}, u32[]{:S(2)}) copy-start(bf16[128,1024]{1,0:T(8,128)(2,1)} %get-tuple-element.216) | copy-start | bytes 786436
  294.1 57.8 %copy-start.5 = (bf16[128,1024]{1,0:T(8,128)(2,1)S(1)}, bf16[128,1024]{1,0:T(8,128)(2,1)}, u32[]{:S(2)}) copy-start(bf16[128,1024]{1,0:T(8,128)(2,1)} %get-tuple-element.215) | copy-start | bytes 786436
  298.4 56.1 %copy-start.11 = (bf16[2,1,128,1024]{3,2,1,0:T(8,128)(2,1)S(1)}, bf16[2,1,128,1024]{3,2,1,0:T(8,128)(2,1)}, u32[]{:S(2)}) copy-start(bf16[2,1,128,1024]{3,2,1,0:T(8,128)(2,1)} %param.19) | copy-start | bytes 1572868
  298.4 86.7 %all-gather.28.cloned.1.call-start = ((), (), s32[]{:S(2)}) async-start(), calls=%async_computation.27 | async-start | bytes 1310720 | tf_op jit(solution)/shard_map/all_gather | solution.py:180
  321.0 33.5 %copy-start.17 = (bf16[128,1024]{1,0:T(8,128)(2,1)S(1)}, bf16[128,1024]{1,0:T(8,128)(2,1)}, u32[]{:S(2)}) copy-start(bf16[128,1024]{1,0:T(8,128)(2,1)} %reduce-scatter.33.cloned.1.call-done) | copy-start | bytes 786436
  358.3 55.8 %all-gather.32.cloned.1.call-start = ((), (), s32[]{:S(2)}) async-start(), calls=%async_computation.33 | async-start | bytes 1310720 | tf_op jit(solution)/shard_map/all_gather | solution.py:180
  359.2 95.2 %reduce-scatter.39.cloned.1.call-start = ((), (), s32[]{:S(2)}) async-start(), calls=%async_computation.28 | async-start | bytes 1310720 | tf_op jit(solution)/shard_map/reduce_scatter | solution.py:188
  426.5 58.6 %reduce-scatter.47.cloned.1.call-start = ((), (), s32[]{:S(2)}) async-start(), calls=%async_computation.34 | async-start | bytes 1310720 | tf_op jit(solution)/shard_map/reduce_scatter | solution.py:188
  426.6 58.6 %copy-start.8 = (bf16[128,1024]{1,0:T(8,128)(2,1)S(1)}, bf16[128,1024]{1,0:T(8,128)(2,1)}, u32[]{:S(2)}) copy-start(bf16[128,1024]{1,0:T(8,128)(2,1)} %reduce-scatter.35.cloned.1.call-done) | copy-start | bytes 786436
  430.8 85.2 %all-gather.34.cloned.1.call-start = ((), (), s32[]{:S(2)}) async-start(), calls=%async_computation.35 | async-start | bytes 1310720 | tf_op jit(solution)/shard_map/all_gather | solution.py:201
  454.4 32.5 %copy-start.41 = (bf16[128,1024]{1,0:T(8,128)(2,1)S(1)}, bf16[128,1024]{1,0:T(8,128)(2,1)}, u32[]{:S(2)}) copy-start(bf16[128,1024]{1,0:T(8,128)(2,1)} %reduce-scatter.39.cloned.1.call-done) | copy-start | bytes 786436
  489.2 55.1 %all-gather.30.cloned.1.call-start = ((), (), s32[]{:S(2)}) async-start(), calls=%async_computation.29 | async-start | bytes 1310720 | tf_op jit(solution)/shard_map/all_gather | solution.py:201
  490.2 107.5 %reduce-scatter.51.cloned.1.call-start = ((), (), s32[]{:S(2)}) async-start(), calls=%async_computation.37 | async-start | bytes 786432 | tf_op jit(solution)/shard_map/reduce_scatter | solution.py:213
  530.6 67.1 %reduce-scatter.49.cloned.1.call-start = ((), (), s32[]{:S(2)}) async-start(), calls=%async_computation.36 | async-start | bytes 786432 | tf_op jit(solution)/shard_map/reduce_scatter | solution.py:210
  540.9 63.8 %reduce-scatter.43.cloned.1.call-start = ((), (), s32[]{:S(2)}) async-start(), calls=%async_computation.31 | async-start | bytes 786432 | tf_op jit(solution)/shard_map/reduce_scatter | solution.py:213
  558.9 45.8 %reduce-scatter.41.cloned.1.call-start = ((), (), s32[]{:S(2)}) async-start(), calls=%async_computation.30 | async-start | bytes 786432 | tf_op jit(solution)/shard_map/reduce_scatter | solution.py:210
  568.9 54.7 %reduce-scatter.63.cloned.1.call-start = ((), (), s32[]{:S(2)}) async-start(), calls=%async_computation.45 | async-start | bytes 294912
  574.7 79.8 %reduce-scatter.65.cloned.1.call-start = ((), (), s32[]{:S(2)}) async-start(), calls=%async_computation.46 | async-start | bytes 294912
  575.7 114.9 %reduce-scatter.61.cloned.1.call-start = ((), (), s32[]{:S(2)}) async-start(), calls=%async_computation.44 | async-start | bytes 2359296
  582.6 144.6 %reduce-scatter.55.cloned.1.call-start = ((), (), s32[]{:S(2)}) async-start(), calls=%async_computation.39 | async-start | bytes 2359296 | tf_op jit(solution)/shard_map/reduce_scatter | solution.py:286
  589.2 169.8 %reduce-scatter.59.cloned.1.call-start = ((), (), s32[]{:S(2)}) async-start(), calls=%async_computation.43 | async-start | bytes 589824
  593.7 194.1 %reduce-scatter.53.cloned.1.call-start = ((), (), s32[]{:S(2)}) async-start(), calls=%async_computation.38 | async-start | bytes 1310720 | tf_op jit(solution)/shard_map/reduce_scatter | solution.py:222
  600.9 217.6 %reduce-scatter.45.cloned.1.call-start = ((), (), s32[]{:S(2)}) async-start(), calls=%async_computation.32 | async-start | bytes 1310720 | tf_op jit(solution)/shard_map/reduce_scatter | solution.py:222
  608.4 246.7 %reduce-scatter.57.cloned.1.call-start = ((), (), s32[]{:S(2)}) async-start(), calls=%async_computation.42 | async-start | bytes 1769472
  618.8 141.9 %copy-start.37 = (bf16[1,512,256]{2,1,0:T(8,128)(2,1)S(1)}, bf16[1,512,256]{2,1,0:T(8,128)(2,1)}, u32[]{:S(2)}) copy-start(bf16[1,512,256]{2,1,0:T(8,128)(2,1)} %copy-done.36) | copy-start | bytes 786436
  618.9 141.9 %copy-start.47 = (bf16[512,256]{1,0:T(8,128)(2,1)S(1)}, bf16[512,256]{1,0:T(8,128)(2,1)}, u32[]{:S(2)}) copy-start(bf16[512,256]{1,0:T(8,128)(2,1)} %reduce-scatter.43.cloned.1.call-done) | copy-start | bytes 786436
  618.9 141.9 %copy-start.49 = (bf16[512,256]{1,0:T(8,128)(2,1)S(1)}, bf16[512,256]{1,0:T(8,128)(2,1)}, u32[]{:S(2)}) copy-start(bf16[512,256]{1,0:T(8,128)(2,1)} %reduce-scatter.41.cloned.1.call-done) | copy-start | bytes 786436
  620.8 167.0 %copy-start.10 = (f32[128,1024]{1,0:T(8,128)S(1)}, f32[128,1024]{1,0:T(8,128)}, u32[]{:S(2)}) copy-start(f32[128,1024]{1,0:T(8,128)} %copy-done.9) | copy-start | bytes 1572868
  (39 other events, 150.2 us)
Sparse Core Ops, SparseCore 0:
  10.4 29.3 all-gather.35
  42.0 27.1 all-gather.17
  71.6 25.7 all-gather.37
  110.9 27.7 reduce-scatter.30
  141.7 27.7 reduce-scatter.34
  170.9 29.1 all-gather.21
  202.6 26.0 all-gather.19
  231.1 26.6 all-gather.25
  259.3 30.8 all-gather.23
  294.2 26.7 reduce-scatter.32
  324.1 27.7 reduce-scatter.36
  358.4 26.6 all-gather.27
  387.5 26.6 all-gather.31
  426.6 27.7 reduce-scatter.38
  457.4 27.7 reduce-scatter.46
  489.4 26.6 all-gather.33
  517.7 26.6 all-gather.29
  547.0 7.9 reduce-scatter.50
  557.9 9.1 reduce-scatter.48
  569.2 9.1 reduce-scatter.42
  580.7 9.0 reduce-scatter.40
  592.0 31.5 reduce-scatter.62
  625.9 28.5 reduce-scatter.64
  656.7 33.8 reduce-scatter.60
  692.9 34.2 reduce-scatter.54
  729.3 29.6 reduce-scatter.58
  761.9 25.8 reduce-scatter.52
  790.7 27.7 reduce-scatter.44
  820.9 34.1 reduce-scatter.56
where the time goes:
time: 874 us; the launch traced here: 864 us
  waiting for transfers between devices  546 us (62%)
  matrix products  125 us (14%)
  blocking collectives  96 us (11%)
  other arithmetic  45.2 us (5%)
  local copies, waits for them, and re-layouts  33.8 us (4%)
  between operations  16.2 us (2%)
    unnamed x34, waiting for transfers between devices  125 us
    reduce_scatter x2, waiting for transfers between devices, backward_pass(): lax.psum_scatter(jnp.einsum('rf,df->rd', d_pre, w_up, preferred_element_t...  54.3 us
    all_gather x2, waiting for transfers between devices, forward_pass(): normed_all = lax.all_gather(normed_rows, 'heads', axis=0, tiled=True)  53.1 us
    reduce_scatter x2, waiting for transfers between devices, forward_pass(): lax.psum_scatter(jnp.dot(hidden, w_down, preferred_element_type=jnp.float...  52.3 us
    all_gather x2, waiting for transfers between devices, backward_pass(): d_mlp_all = lax.all_gather(d_mlp, 'heads', axis=0, tiled=True)  50.2 us
    reduce_scatter x2, waiting for transfers between devices, backward_pass(): lax.psum_scatter(jnp.einsum('trc,tdc->rd', d_qkv, w_qkv, preferred_elemen...  41.1 us
    reduce_scatter x1, waiting for transfers between devices, local(): lax.psum_scatter(grads_total[3].astype(jnp.bfloat16), ('dp', 'seq'), scat...  34.6 us
    all_gather x2, waiting for transfers between devices, backward_pass(): d_attn_all = lax.all_gather(d_attn, 'heads', axis=0, tiled=True)  29.2 us
  transfers between devices with their start and end apart: 29, of which 23 were waited for; matrix products, arithmetic and copies ran while one was open for 18% of the time, Pallas kernels for 0%

commit v1 on v0

v1 whole, which is shorter than its diff:
```python
import functools

import jax
import jax.numpy as jnp
from jax import lax
from jax.experimental import pallas as pl
from jax.experimental.pallas import tpu as pltpu
from jax.sharding import PartitionSpec as P

EPSILON = 1e-05
F32 = jnp.float32
BF16 = jnp.bfloat16
MESH = pl.DeviceIdType.MESH
VMEM_SPEC = pl.BlockSpec(memory_space=pltpu.VMEM)
VMEM_LIMIT = 48 * 1024 * 1024


def dot(left, right, dims):
    return lax.dot_general(left, right, (dims, ((), ())), preferred_element_type=F32)


NN = ((1,), (0,))
NT = ((1,), (1,))
TN = ((0,), (0,))


def norm_parts(rows):
    centred = rows - jnp.mean(rows, -1, keepdims=True)
    spread = jnp.mean(centred * centred, -1, keepdims=True)
    scale = lax.rsqrt(spread + EPSILON)
    return centred * scale, scale


def norm_back(grad, unit, scale, gain):
    inner = grad * gain
    mean_one = jnp.mean(inner, -1, keepdims=True)
    mean_two = jnp.mean(inner * unit, -1, keepdims=True)
    return scale * (inner - mean_one - unit * mean_two)


def row_sum(rows):
    return jnp.sum(rows, 0, keepdims=True)


def exchange_kernel(n, parts, has_sum, has_send, tail, work, n_in, n_out, *refs):
    refs = list(refs)
    partial = refs.pop(0) if has_sum else None
    ins = [refs.pop(0) for _ in range(n_in)]
    gathered = refs.pop(0) if has_send else None
    outs = [refs.pop(0) for _ in range(n_out)]
    relay = n == 4
    if has_sum:
        landing, sum_send, sum_recv = refs.pop(0), refs.pop(0), refs.pop(0)
        if relay:
            relay_in, relay_out, relay_send, relay_recv = [refs.pop(0) for _ in range(4)]
    if has_send:
        all_send, all_recv = refs.pop(0), refs.pop(0)
    if tail:
        tail_land, tail_send, tail_recv = refs.pop(0), refs.pop(0), refs.pop(0)
    me = lax.axis_index("heads")

    def start(src, dst, send_sem, recv_sem, k):
        copy = pltpu.make_async_remote_copy(
            src_ref=src,
            dst_ref=dst,
            send_sem=send_sem,
            recv_sem=recv_sem,
            device_id={"heads": me ^ k},
            device_id_type=MESH,
        )
        copy.start()
        return copy

    barrier = pltpu.get_barrier_semaphore()
    for k in range(1, n):
        pl.semaphore_signal(barrier, inc=1, device_id={"heads": me ^ k}, device_id_type=MESH)
    pl.semaphore_wait(barrier, n - 1)

    own = (partial if has_sum else gathered).shape[2]
    halves = (pl.ds(0, own // 2), pl.ds(own // 2, own // 2))
    started = []
    sums = {}
    relays = {}
    if has_sum and relay:
        for part in range(parts):
            for k in (1, 2):
                relays[part, k] = start(
                    partial.at[part, me ^ 3, halves[k - 1]],
                    relay_in.at[part, k - 1],
                    relay_send.at[part, k - 1],
                    relay_recv.at[part, k - 1],
                    k,
                )
            for k in (1, 2):
                half = halves[k - 1]
                sums[part, k, 0] = start(
                    partial.at[part, me ^ k, half],
                    landing.at[part, k - 1, half],
                    sum_send.at[part, k - 1],
                    sum_recv.at[part, k - 1],
                    k,
                )
        for part in range(parts):
            for k in (1, 2):
                other, half = 3 - k, halves[k - 1]
                relays[part, k].wait_recv()
                relay_out[part, k - 1] = (
                    partial[part, me ^ other, half].astype(F32)
                    + relay_in[part, k - 1].astype(F32)
                ).astype(BF16)
                sums[part, other, 1] = start(
                    relay_out.at[part, k - 1],
                    landing.at[part, other - 1, half],
                    sum_send.at[part, 1 + other],
                    sum_recv.at[part, 1 + other],
                    other,
                )
    elif has_sum:
        for part in range(parts):
            for k in range(1, n):
                sums[part, k, 0] = start(
                    partial.at[part, me ^ k],
                    landing.at[part, k - 1],
                    sum_send.at[part, k - 1],
                    sum_recv.at[part, k - 1],
                    k,
                )
    neighbours = (1, 2) if relay else tuple(range(1, n))
    sends = {}
    for part in range(parts):
        total = None
        if has_sum:
            total = partial[part, me].astype(F32)
            for k in neighbours:
                sums[part, k, 0].wait_recv()
                if relay:
                    sums[part, k, 1].wait_recv()
                total = total + landing[part, k - 1].astype(F32)
        passed = work(part, total, ins, outs)
        if has_send:
            gathered[part, me] = passed
            for k in neighbours:
                sends[part, k] = start(
                    gathered.at[part, me],
                    gathered.at[part, me],
                    all_send.at[part, k - 1],
                    all_recv.at[part, k - 1],
                    k,
                )
    if tail:
        mine = [sum(ref[part] for part in range(parts)) for ref in (outs[1], ins[-1])]
        tail_land[me] = jnp.concatenate(mine + [jnp.zeros((2, mine[0].shape[1]), F32)], 0)
        tails = [
            start(tail_land.at[me], tail_land.at[me], tail_send.at[k - 1], tail_recv.at[k - 1], k)
            for k in range(1, n)
        ]
    if has_send and relay:
        for part in range(parts):
            for k in (1, 2):
                sends[part, k].wait_recv()
                half = halves[k - 1]
                other = 3 - k
                started.append(
                    start(
                        gathered.at[part, me ^ k, half],
                        gathered.at[part, me ^ k, half],
                        all_send.at[part, 1 + other],
                        all_recv.at[part, 1 + other],
                        other,
                    )
                )
        for copy in started:
            copy.wait_recv()
    elif has_send:
        for copy in sends.values():
            copy.wait_recv()
    if tail:
        for copy in tails:
            copy.wait_recv()
        outs[-1][...] = sum(tail_land[k, 0:6] for k in range(n))
        for copy in tails:
            copy.wait_send()
    for copy in list(relays.values()) + list(sums.values()) + list(sends.values()) + started:
        copy.wait_send()


def exchange(n, name, ident, work, partial, ins, out_shapes, has_send, shape, tail=False):
    parts, rows, width = shape
    has_sum = partial is not None
    relay = n == 4
    operands = ([partial] if has_sum else []) + list(ins)
    shapes = ([jax.ShapeDtypeStruct((parts, n, rows, width), BF16)] if has_send else []) + [
        jax.ShapeDtypeStruct(s, t) for s, t in out_shapes
    ]
    sems = pltpu.SemaphoreType.DMA((parts, 4 if relay else n - 1))
    scratch = []
    if has_sum:
        scratch += [pltpu.VMEM((parts, 2 if relay else n - 1, rows, width), BF16), sems, sems]
        if relay:
            scratch += [pltpu.VMEM((parts, 2, rows // 2, width), BF16)] * 2
            scratch += [pltpu.SemaphoreType.DMA((parts, 2))] * 2
    if has_send:
        scratch += [sems, sems]
    if tail:
        scratch += [pltpu.VMEM((n, 8, width), F32)] + [pltpu.SemaphoreType.DMA((n - 1,))] * 2
    return pl.pallas_call(
        functools.partial(
            exchange_kernel, n, parts, has_sum, has_send, tail, work, len(ins), len(out_shapes)
        ),
        out_shape=shapes,
        in_specs=[VMEM_SPEC] * len(operands),
        out_specs=[VMEM_SPEC] * len(shapes),
        scratch_shapes=scratch,
        compiler_params=pltpu.CompilerParams(
            collective_id=ident, has_side_effects=True, vmem_limit_bytes=VMEM_LIMIT
        ),
        cost_estimate=pl.CostEstimate(
            flops=1000000, bytes_accessed=60000000, transcendentals=0
        ),
        name=name,
    )(*operands)


def work_inputs(part, total, ins, outs):
    return ins[0][part]


def work_first(part, total, ins, outs):
    x_rows, gains, shifts = ins
    first = x_rows[part].astype(F32) + total + shifts[0:1]
    outs[0][part] = first
    unit, _ = norm_parts(first)
    normed = (unit * gains[0:1] + shifts[1:2]).astype(BF16)
    outs[1][part] = normed
    return normed


def work_second(part, total, ins, outs):
    normed, cotangent, gains, shifts = ins
    second = normed[part].astype(F32) + total + shifts[2:3]
    unit, scale = norm_parts(second)
    outs[0][part] = (unit * gains[1:2] + shifts[3:4]).astype(BF16)
    grad = cotangent[part].astype(F32)
    d_second = norm_back(grad, unit, scale, gains[1:2])
    outs[1][part] = d_second
    low = d_second.astype(BF16)
    sums = jnp.concatenate(
        [row_sum(grad * unit), row_sum(low.astype(F32)), row_sum(grad)], 0
    )
    outs[2][part] = sums
    return low


def work_third(part, total, ins, outs):
    first, d_second, gains, _ = ins
    grad = total + d_second[part]
    unit, scale = norm_parts(first[part])
    d_first = norm_back(grad, unit, scale, gains[0:1])
    outs[0][part] = d_first
    low = d_first.astype(BF16)
    sums = jnp.concatenate(
        [row_sum(grad * unit), row_sum(low.astype(F32)), row_sum(grad)], 0
    )
    outs[1][part] = sums
    return low


def work_last(part, total, ins, outs):
    outs[0][part] = (total + ins[0][part]).astype(BF16)
    return None


def attend_kernel(head, q_ref, k_ref, v_ref, k_far, v_far, o_ref, log_ref):
    queries = q_ref[0] * jnp.asarray(0.125, BF16)
    keys = jnp.concatenate([k_ref[0], k_far[0]], 0)
    values = jnp.concatenate([v_ref[0], v_far[0]], 0)
    mixed, logs = [], []
    for h in range(q_ref.shape[-1] // head):
        cols = slice(h * head, (h + 1) * head)
        scores = dot(keys[:, cols], queries[:, cols], NT)
        largest = jnp.max(scores, 0, keepdims=True)
        weights = jnp.exp(scores - largest)
        totals = jnp.sum(weights, 0, keepdims=True)
        probs = (weights * (1.0 / totals)).astype(BF16)
        mixed.append(dot(probs, values[:, cols], TN))
        logs.append(largest + jnp.log(totals))
    o_ref[0] = jnp.concatenate(mixed, -1).astype(BF16)
    log_ref[0, 0] = jnp.concatenate(logs, 0)


def attend_back_kernel(
    head, q_ref, k_ref, v_ref, k_far, v_far, do_ref, log_ref, dq_ref, dkv_ref, far_ref
):
    half = k_ref.shape[1]
    queries = q_ref[0] * jnp.asarray(0.125, BF16)
    keys = jnp.concatenate([k_ref[0], k_far[0]], 0)
    values = jnp.concatenate([v_ref[0], v_far[0]], 0)
    d_mixed = do_ref[0]
    dq, dk, dv = [], [], []
    for h in range(q_ref.shape[-1] // head):
        cols = slice(h * head, (h + 1) * head)
        scores = dot(keys[:, cols], queries[:, cols], NT)
        probs = jnp.exp(scores - log_ref[0, 0, h : h + 1])
        d_probs = dot(values[:, cols], d_mixed[:, cols], NT)
        centre = jnp.sum(probs * d_probs, 0, keepdims=True)
        d_scores = (probs * (d_probs - centre)).astype(BF16)
        dv.append(dot(probs.astype(BF16), d_mixed[:, cols], NN))
        dk.append(dot(d_scores, queries[:, cols], NN))
        dq.append(dot(d_scores, keys[:, cols], TN) * 0.125)
    dq_ref[0] = jnp.concatenate(dq, -1).astype(BF16)
    for at, rows in enumerate((dk, dv)):
        rows = jnp.concatenate(rows, -1)
        dkv_ref[at, 0] = rows[:half]
        far_ref[at, 0] = rows[half:].astype(BF16)


def attention_call(kernel, name, queries, kv, kv_far, more, more_logs, outs, dots, head):
    micro, rows, width = queries.shape
    half = kv.shape[1]
    block = min(128, width)
    blocks = width // block
    row_spec = pl.BlockSpec((1, rows, block), lambda m, j: (m, 0, j))
    log_spec = pl.BlockSpec((1, 1, block // head, rows), lambda m, j: (m, j, 0, 0))
    pair_spec = pl.BlockSpec((2, 1, half, block), lambda m, j: (0, m, 0, j))
    shared = block % 128 == 0
    skip = blocks if shared else 0
    value_spec = pl.BlockSpec((1, half, block), lambda m, j: (m, 0, j + skip))
    both = [(v, v) if shared else (v[..., :width], v[..., width:]) for v in (kv, kv_far)]
    kinds = {
        "row": (row_spec, jax.ShapeDtypeStruct(queries.shape, BF16)),
        "log": (log_spec, jax.ShapeDtypeStruct((micro, blocks, block // head, rows), F32)),
        "pair": (pair_spec, jax.ShapeDtypeStruct((2, micro, half, width), F32)),
        "far": (pair_spec, jax.ShapeDtypeStruct((2, micro, half, width), BF16)),
    }
    return pl.pallas_call(
        functools.partial(kernel, head),
        grid=(micro, blocks),
        in_specs=[row_spec] + [row_spec, value_spec] * 2
        + [row_spec] * len(more) + [log_spec] * len(more_logs),
        out_specs=[kinds[k][0] for k in outs],
        out_shape=[kinds[k][1] for k in outs],
        compiler_params=pltpu.CompilerParams(vmem_limit_bytes=VMEM_LIMIT),
        cost_estimate=pl.CostEstimate(
            flops=2 * dots * micro * rows * 2 * half * width * 4,
            bytes_accessed=20000000,
            transcendentals=0,
        ),
        name=name,
    )(queries, *both[0], *both[1], *more, *more_logs)


def gelu_parts(value):
    cdf = 0.5 * (1.0 + lax.erf(value * 0.7071067811865476))
    return cdf, 0.3989422804014327 * jnp.exp(-0.5 * value * value)


def local(inputs, w_qkv, b_qv, w_out, w_up, b_up, w_down, ln_gains, ln_shifts, cotangent):
    n = lax.axis_size("heads")
    owners = lax.axis_size("dp") * lax.axis_size("seq")
    share = ("dp", "seq")
    micro, _, own, width = inputs.shape
    rows = n * own
    heads_here, head = b_qv.shape[1], b_qv.shape[2] * owners
    cols = heads_here * head
    depth = w_qkv.shape[1]
    hidden_here = w_up.shape[1]
    piece = (micro, own, width)

    small = jnp.concatenate([v.reshape(-1) for v in (b_qv, b_up, ln_gains, ln_shifts)])
    small_rows = -(-small.size // (3 * cols * 16)) * 16
    small = jnp.pad(small, (0, small_rows * 3 * cols - small.size)).reshape(small_rows, 3 * cols)
    qkv_mine = jnp.concatenate([jnp.swapaxes(w_qkv, 0, 1).reshape(depth, 3 * cols), small], 0)
    qkv_all = lax.all_gather(qkv_mine, share, axis=0, tiled=False)
    x_rows = inputs[:, 0]
    (gathered,) = exchange(n, "gather_inputs", 0, work_inputs, None, [x_rows], [], True, piece)
    gathered = gathered.reshape(micro * rows, width)
    out_all = lax.all_gather(w_out.T, share, axis=0, tiled=True)
    up_all = lax.all_gather(w_up, share, axis=0, tiled=True)
    down_all = lax.all_gather(w_down.T, share, axis=0, tiled=True)

    q_weights = qkv_all[:, :depth, :cols].reshape(owners * depth, cols)
    kv_weights = qkv_all[:, :depth, cols:].reshape(owners * depth, 2 * cols)
    small_all = qkv_all[:, depth:].reshape(owners, -1)
    at = 0
    pieces = []
    for v in (b_qv, b_up, ln_gains, ln_shifts):
        part = small_all[:, at : at + v.size].reshape((owners,) + v.shape)
        pieces.append(jnp.moveaxis(part, 0, -2).reshape(v.shape[:-1] + (-1,)).astype(F32))
        at += v.size
    bias_qv, bias_up, gains, shifts = pieces
    bias_qv = bias_qv.reshape(2, cols)
    bias_kv = jnp.concatenate([jnp.zeros_like(bias_qv[0]), bias_qv[1]])
    swap = [(0, 1), (1, 0)]

    kv = (dot(gathered, kv_weights, NN) + bias_kv).astype(BF16).reshape(micro, rows, 2 * cols)
    kv_far = lax.ppermute(kv, "seq", swap)
    queries = (dot(gathered, q_weights, NN) + bias_qv[0]).astype(BF16).reshape(micro, rows, cols)
    mixed, logs = attention_call(
        attend_kernel, "attend", queries, kv, kv_far, [], [], ["row", "log"], 2, head
    )
    mixed_rows = mixed.reshape(micro * rows, cols)
    partial = dot(mixed_rows, out_all, NT).astype(BF16).reshape(micro, n, own, width)
    normed_all, first, normed = exchange(
        n, "first_norm", 1, work_first, partial, [x_rows, gains, shifts],
        [(piece, F32), (piece, BF16)], True, piece,
    )
    normed_all = normed_all.reshape(micro * rows, width)
    hidden_pre = dot(normed_all, up_all, NN) + bias_up.reshape(-1)
    cdf, density = gelu_parts(hidden_pre)
    hidden = (hidden_pre * cdf).astype(BF16)
    slope = cdf + hidden_pre * density
    partial = dot(hidden, down_all, NT).astype(BF16).reshape(micro, n, own, width)
    d_mlp, result, d_second, sums_two = exchange(
        n, "second_norm", 2, work_second, partial, [normed, cotangent[:, 0], gains, shifts],
        [(piece, BF16), (piece, F32), ((micro, 3, width), F32)], True, piece,
    )

    d_mlp = d_mlp.reshape(micro * rows, width)
    d_pre_wide = dot(d_mlp, down_all, NN) * slope
    d_pre = d_pre_wide.astype(BF16)
    partial = dot(d_pre, up_all, NT).astype(BF16).reshape(micro, n, own, width)
    g_down = dot(d_mlp, hidden, TN).astype(BF16)
    g_up = dot(normed_all, d_pre, TN).astype(BF16)
    g_bup = jnp.sum(d_pre.astype(F32), 0).reshape(b_up.shape[0], owners, b_up.shape[1])
    g_bup = jnp.swapaxes(g_bup, 0, 1).reshape(owners, -1)

    def with_extra(wide, extra):
        wide = wide.reshape(owners, -1, wide.shape[-1])
        span = wide.shape[-1]
        extra = jnp.pad(extra, ((0, 0), (0, -extra.shape[-1] % (16 * span)))).astype(BF16)
        return jnp.concatenate([wide, extra.reshape(owners, -1, span)], 1)

    g_up = with_extra(g_up, g_bup)
    partial, g_down, g_up = lax.optimization_barrier((partial, g_down, g_up))
    g_down = lax.psum_scatter(g_down, share, scatter_dimension=0, tiled=True)
    g_up = lax.psum_scatter(g_up, share, scatter_dimension=0, tiled=False)
    d_attn, d_first, _, norm_sums = exchange(
        n, "first_norm_back", 3, work_third, partial, [first, d_second, gains, sums_two],
        [(piece, F32), ((micro, 3, width), F32), ((6, width), F32)], True, piece, tail=True,
    )

    d_attn = d_attn.reshape(micro * rows, width)
    d_mixed = dot(d_attn, out_all, NN).astype(BF16).reshape(micro, rows, cols)
    norm_sums = jnp.swapaxes(norm_sums.reshape(6, owners, depth), 0, 1).reshape(owners, -1)
    g_out = with_extra(dot(d_attn, mixed_rows, TN).astype(BF16), norm_sums)
    d_mixed, g_out = lax.optimization_barrier((d_mixed, g_out))
    g_out = lax.psum_scatter(g_out, share, scatter_dimension=0, tiled=False)
    d_query, d_kv, d_far = attention_call(
        attend_back_kernel, "attend_back", queries, kv, kv_far, [d_mixed], [logs],
        ["row", "pair", "far"], 5, head,
    )
    d_kv = (d_kv + lax.ppermute(d_far, "seq", swap).astype(F32)).astype(BF16)
    d_qkv = jnp.concatenate([d_query, d_kv[0], d_kv[1]], -1).reshape(micro * rows, 3 * cols)
    qkv_weights = qkv_all[:, :depth].reshape(owners * depth, 3 * cols)
    partial = dot(d_qkv, qkv_weights, NT).astype(BF16).reshape(micro, n, own, width)
    sums = jnp.sum(d_qkv.astype(F32), 0).reshape(3, heads_here, owners, head // owners)
    g_bqv = jnp.moveaxis(jnp.stack([sums[0], sums[2]]), 2, 0).reshape(owners, -1)
    g_qkv = with_extra(dot(gathered, d_qkv, TN).astype(BF16), g_bqv)
    partial, g_qkv = lax.optimization_barrier((partial, g_qkv))
    g_qkv = lax.psum_scatter(g_qkv, share, scatter_dimension=0, tiled=False)
    (d_inputs,) = exchange(
        n, "input_grad", 4, work_last, partial, [d_first], [(piece, BF16)], False, piece
    )

    norm_mine = g_out[depth:].reshape(-1)[: 6 * depth].astype(F32).reshape(6, depth)
    gain_grad = jnp.stack([norm_mine[0], norm_mine[3]])
    shift_grad = jnp.stack([norm_mine[1], norm_mine[2], norm_mine[4], norm_mine[5]])
    qkv_grad = jnp.swapaxes(g_qkv[:depth].astype(F32).reshape(depth, 3, cols), 0, 1)
    bqv_grad = g_qkv[depth:].reshape(-1)[: b_qv.size].astype(F32).reshape(b_qv.shape)
    up_grad = g_up[:depth].astype(F32)
    bup_grad = g_up[depth:].reshape(-1)[: b_up.size].astype(F32).reshape(b_up.shape)
    return (
        result[:, None],
        d_inputs[:, None],
        qkv_grad,
        bqv_grad,
        g_out[:depth].astype(F32).T,
        up_grad,
        bup_grad,
        g_down.astype(F32).T,
        gain_grad,
        shift_grad,
    )


def solution(mesh):
    rows_spec = P(None, "dp", ("seq", "heads"), None)
    weight_specs = (
        P(None, ("dp", "seq"), "heads"),
        P(None, "heads", ("dp", "seq")),
        P("heads", ("dp", "seq")),
        P(("dp", "seq"), "heads"),
        P("heads", ("dp", "seq")),
        P("heads", ("dp", "seq")),
        P(None, ("dp", "seq")),
        P(None, ("dp", "seq")),
    )
    return jax.shard_map(
        local,
        mesh=mesh,
        in_specs=(rows_spec,) + weight_specs + (rows_spec,),
        out_specs=(rows_spec, rows_spec) + weight_specs,
        check_vma=False,
    )
```

time: 874 us -> 417 us (0.48)
  waiting for transfers between devices: 546 us -> 89.1 us
  Pallas kernels: 0 us -> 188 us
  blocking collectives: 96 us -> 18.8 us
  matrix products: 125 us -> 50.4 us
  other arithmetic: 45.2 us -> 14.9 us
    all_gather x11 -> x3, waiting for transfers between devices: 212 us -> 5.76 us  [the longest x1 5.76 us: local(): qkv_all = lax.all_gather(qkv_mine, share, axis=0, tiled=False)]
    pallas_call x0 -> x7, Pallas kernels: none -> 188 us  [the longest x5 162 us: exchange(): pl.pallas_call(functools.partial(exchange_kernel, n, parts, has_sum, has_...]
    reduce_scatter x13 -> x4, waiting for transfers between devices: 209 us -> 79.4 us  [the longest x1 39.4 us: local(): g_qkv = lax.psum_scatter(g_qkv, share, scatter_dimension=0, tiled=False)]
    unnamed x34 -> x7, waiting for transfers between devices: 125 us -> 2.66 us
    dot_general x36 -> x13, matrix products: 125 us -> 50.4 us  [dot(): lax.dot_general(left, right, (dims, ((), ())), preferred_element_type=F32)]
    all_gather x9 -> x1, blocking collectives: 71.8 us -> 18.8 us  [local(): out_all = lax.all_gather(w_out.T, share, axis=0, tiled=True)]
    reduce_sum x19 -> x1, other arithmetic: 19.9 us -> 0.29 us  [local(): jnp.sum(d_qkv.astype(F32), 0).reshape(3, heads_here, owners, head // owners)]
    convert_element_type x12 -> x7, other arithmetic: 20.2 us -> 2.74 us  [the longest x1 1.79 us: local(): up_grad = g_up[:depth].astype(F32)]
  transfers between devices with their start and end apart: 29 -> 9, of which waited for: 23 -> 5; matrix products, arithmetic and copies ran while one was open for 18% -> 11% of each run, Pallas kernels for 0% -> 26%
where the time goes in v1:
time: 417 us; the launch traced here: 413 us
  Pallas kernels  188 us (45%)
  waiting for transfers between devices  89.1 us (21%)
  matrix products  50.4 us (12%)
  local copies, waits for them, and re-layouts  35.5 us (9%)
  blocking collectives  18.8 us (5%)
  between operations  15.1 us (4%)
  other arithmetic  14.9 us (4%)
    pallas_call x5, Pallas kernels, exchange(): pl.pallas_call(functools.partial(exchange_kernel, n, parts, has_sum, has_...  162 us
    dot_general x13, matrix products, dot(): lax.dot_general(left, right, (dims, ((), ())), preferred_element_type=F32)  50.4 us
    reduce_scatter x1, waiting for transfers between devices, local(): g_qkv = lax.psum_scatter(g_qkv, share, scatter_dimension=0, tiled=False)  39.4 us
    reduce_scatter x1, waiting for transfers between devices, local(): g_up = lax.psum_scatter(g_up, share, scatter_dimension=0, tiled=False)  33.8 us
    pallas_call x2, Pallas kernels, attention_call(): pl.pallas_call(functools.partial(kernel, head), grid=(micro, blocks), in_...  26.8 us
    all_gather x1, blocking collectives, local(): out_all = lax.all_gather(w_out.T, share, axis=0, tiled=True)  18.8 us
    unnamed x75, local copies, waits for them, and re-layouts  17.6 us
  transfers between devices with their start and end apart: 9, of which 5 were waited for; matrix products, arithmetic and copies ran while one was open for 11% of the time, Pallas kernels for 26%

profile of v1, /device:TPU:0, one launch (start us, length us, event | category | flops | bytes accessed | tf_op | source)
XLA Modules:
  0.0 412.7 jit_solution(15651042079225200987)
XLA Ops:
  9.9 1.1 copy.135
  13.5 21.9 %gather_inputs.1 = bf16[2,4,128,1024]{3,2,1,0:T(8,128)(2,1)S(1)} custom-call(bf16[2,128,1024]{2,1,0:T(8,128)(2,1)S(1)} %bitcast.155), custom_call_target="tpu_custom_call" | custom-call | flops 1000000 | bytes 60000000 | tf_op jit(solution)/shard_map/gather_inputs/pallas_call | solution.py:206
  35.4 5.8 %all-gather.9.cloned.1.call-done = bf16[1152,768]{1,0:T(8,128)(2,1)} async-done(((bf16[144,768]{1,0:T(8,128)(2,1)}), bf16[1152,768]{1,0:T(8,128)(2,1)}) %all-gather.9.cloned.1.call-update) | async-done | bytes 1769488 | tf_op jit(solution)/shard_map/all_gather | solution.py:373
  41.2 2.3 slice.187
  43.4 0.9 slice_bitcast_fusion.1
  44.7 3.6 fusion.7
  48.2 2.3 copy.141
  50.8 18.8 %all_gather.17 = bf16[1024,256]{0,1:T(8,128)(2,1)} all-gather(bf16[128,256]{0,1:T(8,128)(2,1)S(1)} %bitcast.220), channel_id=1, replica_groups=mesh['dp'=4,'seq'=2,'heads'=4] {'dp','seq'}, dimensions={0}, use_global_device_ids=true | all-gather | bytes 589824 | tf_op jit(solution)/shard_map/all_gather | solution.py:377
  69.6 1.1 slice.183
  71.3 1.6 fusion.9
  72.9 1.2 copy.140
  74.1 1.4 copy-done.3
  75.6 11.1 %attend.1 = (bf16[2,512,256]{2,1,0:T(8,128)(2,1)S(1)}, f32[2,2,2,512]{3,2,1,0:T(2,128)S(1)}) custom-call(bf16[2,512,256]{2,1,0:T(8,128)(2,1)S(1)} %bitcast.168, bf16[2,512,512]{2,1,0:T(8,128)(2,1)S(1)} %bitcast.163, bf16[2,512,512]{2,1,0:T(8,128)(2,1)S(1)} %bitcast.164, bf16[2,512,512]{2,1,0:T(8,128)(2,1)} %collective-permute-done.k_far.v_far, ...), custom_call_target="tpu_custom_call" | custom-call | flops 4294967296 | bytes 20000000 | tf_op jit(solution)/shard_map/attend/pallas_call | solution.py:335
  86.7 2.1 convolution_convert_fusion.4
  88.8 39.5 %first_norm.1 = (bf16[2,4,128,1024]{3,2,1,0:T(8,128)(2,1)S(1)}, f32[2,128,1024]{2,1,0:T(8,128)S(1)}, bf16[2,128,1024]{2,1,0:T(8,128)(2,1)S(1)}) custom-call(bf16[2,4,128,1024]{3,2,1,0:T(8,128)(2,1)} %bitcast.186, bf16[2,128,1024]{2,1,0:T(8,128)(2,1)S(1)} %bitcast.156, f32[2,1024]{1,0:T(2,128)S(1)} %bitcast.178, f32[4,1024]{1,0:T(4,128)S(1)} %bitcast.176), custom_call_target="tpu_custom_call" | custom-call | flops 1000000 | bytes 60000000 | tf_op jit(solution)/shard_map/first_norm/pallas_call | solution.py:206
  128.3 1.0 copy-done.5
  130.1 1.4 copy-done.18
  131.4 7.4 %multiply_convert_fusion = (bf16[1024,1024]{1,0:T(8,128)(2,1)}, f32[1024,1024]{1,0:T(8,128)}) fusion(f32[1024]{0:T(1024)S(1)} %reshape.260, bf16[1024,1024]{1,0:T(8,128)(2,1)} %bitcast.181, bf16[1024,1024]{1,0:T(8,128)(2,1)} %all-gather.5.cloned.1.call-done), kind=kOutput, calls=%fused_computation.7 | convolution fusion | flops 2153775104 | bytes 10489856 | tf_op jit(solution)/shard_map/dot_general | solution.py:19
  138.9 6.0 %convolution_convert_fusion.3 = bf16[1024,1024]{1,0:T(8,128)(2,1)} fusion(bf16[1024,1024]{1,0:T(8,128)(2,1)} %get-tuple-element.136, bf16[1024,1024]{0,1:T(8,128)(2,1)} %all-gather.7.cloned.1.call-done), kind=kOutput, calls=%fused_computation.16 | convolution fusion | flops 2148532224 | bytes 6291456 | tf_op jit(solution)/shard_map/dot_general | solution.py:19
  144.9 40.2 %second_norm.1 = (bf16[2,4,128,1024]{3,2,1,0:T(8,128)(2,1)}, bf16[2,128,1024]{2,1,0:T(8,128)(2,1)S(1)}, f32[2,128,1024]{2,1,0:T(8,128)S(1)}, f32[2,3,1024]{2,1,0:T(4,128)S(1)}) custom-call(bf16[2,4,128,1024]{3,2,1,0:T(8,128)(2,1)} %bitcast.192, bf16[2,128,1024]{2,1,0:T(8,128)(2,1)S(1)} %copy-done.17, bf16[2,128,1024]{2,1,0:T(8,128)(2,1)S(1)} %bitcast.173, ...), custom_call_target="tpu_custom_call" | custom-call | flops 1000000 | bytes 60000000 | tf_op jit(solution)/shard_map/second_norm/pallas_call | solution.py:206
  185.1 1.0 copy-done.7
  186.0 5.3 %convolution_convert_fusion.1 = bf16[1024,1024]{1,0:T(8,128)(2,1)} fusion(bf16[1024,1024]{1,0:T(8,128)(2,1)} %bitcast.28, bf16[1024,1024]{1,0:T(8,128)(2,1)S(1)} %copy-done.28), kind=kOutput, calls=%fused_computation.14 | convolution fusion | flops 2148532224 | bytes 6291456 | tf_op jit(solution)/shard_map/dot_general | solution.py:19
  191.4 6.8 %fusion.23 = (bf16[1024]{0:T(1024)(128)(2,1)S(1)}, bf16[1024,1024]{1,0:T(8,128)(2,1)S(1)}) fusion(f32[1024,1024]{1,0:T(8,128)} %get-tuple-element.137, f32[1024]{0:T(1024)S(1)} %reshape.260, bf16[1024,1024]{1,0:T(8,128)(2,1)} %bitcast.28, bf16[1024,1024]{0,1:T(8,128)(2,1)} %all-gather.7.cloned.1.call-done), kind=kOutput, calls=%fused_computation.76 | convolution fusion | flops 2160065536 | bytes 10491904 | tf_op jit(solution)/shard_map/dot_general | solution.py:19
  198.2 3.8 convolution_convert_fusion
  202.4 3.2 pad_maximum_fusion.1
  205.7 6.1 %convolution_convert_fusion.2 = bf16[1024,1024]{1,0:T(8,128)(2,1)} fusion(bf16[1024,1024]{1,0:T(8,128)(2,1)} %copy-done.29, bf16[1024,1024]{1,0:T(8,128)(2,1)} %all-gather.5.cloned.1.call-done), kind=kOutput, calls=%fused_computation.15 | convolution fusion | flops 2148532224 | bytes 6291456 | tf_op jit(solution)/shard_map/dot_general | solution.py:19
  211.8 39.2 %first_norm_back.1 = (bf16[2,4,128,1024]{3,2,1,0:T(8,128)(2,1)S(1)}, f32[2,128,1024]{2,1,0:T(8,128)S(1)}, f32[2,3,1024]{2,1,0:T(4,128)}, f32[6,1024]{1,0:T(8,128)S(1)}) custom-call(bf16[2,4,128,1024]{3,2,1,0:T(8,128)(2,1)} %bitcast.194, f32[2,128,1024]{2,1,0:T(8,128)S(1)} %copy-done.6, f32[2,128,1024]{2,1,0:T(8,128)S(1)} %copy-done.8, ...), custom_call_target="tpu_custom_call" | custom-call | flops 1000000 | bytes 60000000 | tf_op jit(solution)/shard_map/first_norm_back/pallas_call | solution.py:206
  252.5 1.5 convolution_convert_fusion.8
  255.6 1.2 copy-done.4
  256.8 1.0 copy-done.20
  257.9 15.7 %attend_back.1 = (bf16[2,512,256]{2,1,0:T(8,128)(2,1)S(1)}, f32[2,2,512,256]{3,2,1,0:T(8,128)}, bf16[2,2,512,256]{3,2,1,0:T(8,128)(2,1)S(1)}) custom-call(bf16[2,512,256]{2,1,0:T(8,128)(2,1)S(1)} %bitcast.169, bf16[2,512,512]{2,1,0:T(8,128)(2,1)S(1)} %bitcast.165, bf16[2,512,512]{2,1,0:T(8,128)(2,1)S(1)} %bitcast.166, ...), custom_call_target="tpu_custom_call" | custom-call | flops 10737418240 | bytes 20000000 | tf_op jit(solution)/shard_map/attend_back/pallas_call | solution.py:335
  273.6 1.4 slice.194
  275.0 1.3 collective-permute-done.1
  276.6 1.8 fusion.6
  279.5 1.5 copy.147
  281.0 3.8 pad_maximum_fusion
  284.7 3.6 convolution_convert_fusion.5
  289.1 1.2 copy-done.2
  290.3 20.7 %input_grad.1 = bf16[2,128,1024]{2,1,0:T(8,128)(2,1)S(1)} custom-call(bf16[2,4,128,1024]{3,2,1,0:T(8,128)(2,1)S(1)} %bitcast.160, f32[2,128,1024]{2,1,0:T(8,128)S(1)} %copy-done.2), custom_call_target="tpu_custom_call" | custom-call | flops 1000000 | bytes 60000000 | tf_op jit(solution)/shard_map/input_grad/pallas_call | solution.py:206
  314.5 6.2 %reduce-scatter.11.cloned.1.call-done = bf16[128,1024]{1,0:T(8,128)(2,1)} async-done(((bf16[1024,1024]{1,0:T(8,128)(2,1)}), bf16[128,1024]{1,0:T(8,128)(2,1)}) %reduce-scatter.11.cloned.1.call-update) | async-done | bytes 262160 | tf_op jit(solution)/shard_map/reduce_scatter | solution.py:435
  320.7 1.0 convert_bitcast_fusion
  321.7 1.0 copy.155
  322.7 39.4 %reduce-scatter.5.cloned.1.call-done = bf16[1,144,768]{1,2,0:T(8,128)(2,1)} async-done(((bf16[8,144,768]{1,2,0:T(8,128)(2,1)}), bf16[1,144,768]{1,2,0:T(8,128)(2,1)}) %reduce-scatter.5.cloned.1.call-update) | async-done | bytes 221200 | tf_op jit(solution)/shard_map/reduce_scatter | solution.py:460
  362.1 0.9 slice.196
  363.2 1.0 slice.195
  364.2 0.9 copy.152
  366.2 33.8 %reduce-scatter.9.cloned.1.call-done = bf16[1,144,1024]{2,1,0:T(8,128)(2,1)} async-done(((bf16[8,144,1024]{2,1,0:T(8,128)(2,1)}), bf16[1,144,1024]{2,1,0:T(8,128)(2,1)}) %reduce-scatter.9.cloned.1.call-update) | async-done | bytes 294928 | tf_op jit(solution)/shard_map/reduce_scatter | solution.py:436
  402.0 1.8 fusion.10
  (138 shorter events, 20.7 us)
Async XLA Ops:
  7.2 6.3 %copy-start = (bf16[2,1,128,1024]{3,2,1,0:T(8,128)(2,1)S(1)}, bf16[2,1,128,1024]{3,2,1,0:T(8,128)(2,1)}, u32[]{:S(2)}) copy-start(bf16[2,1,128,1024]{3,2,1,0:T(8,128)(2,1)} %param.10) | copy-start | bytes 1572868
  7.2 34.0 %all-gather.9.cloned.1.call-start = ((), (), s32[]{:S(2)}) async-start(), calls=%async_computation.10 | async-start | bytes 1990656 | tf_op jit(solution)/shard_map/all_gather | solution.py:373
  11.9 119.5 %all-gather.5.cloned.1.call-start = ((), (), s32[]{:S(2)}) async-start(), calls=%async_computation.4 | async-start | bytes 2359296 | tf_op jit(solution)/shard_map/all_gather | solution.py:378
  12.7 126.2 %all-gather.7.cloned.1.call-start = ((), (), s32[]{:S(2)}) async-start(), calls=%async_computation.5 | async-start | bytes 2359296 | tf_op jit(solution)/shard_map/all_gather | solution.py:379
  13.4 297.6 %reduce-scatter.7.cloned.1.call-start = ((), (), s32[]{:S(2)}) async-start(), calls=%async_computation.7 | async-start | bytes 663552 | tf_op jit(solution)/shard_map/reduce_scatter | solution.py:447
  48.2 2.6 copy-start.27
  50.6 23.5 %collective-permute-start = (bf16[2,512,512]{2,1,0:T(8,128)(2,1)}, bf16[2,512,512]{2,1,0:T(8,128)(2,1)}, u32[]{:S(2)}, u32[]{:S(2)}) collective-permute-start(bf16[2,512,512]{2,1,0:T(8,128)(2,1)} %bitcast.162), channel_id=1, source_target_pairs={{0,4},{4,0},{1,5},{5,1},{2,6},{6,2},{3,7},{7,3},{8,12},{12,8},{9,1... | collective-permute-start | bytes 3145736 | tf_op jit(solution)/shard_map/ppermute | solution.py:396
  74.1 12.5 %copy-start.9 = (bf16[1024,256]{1,0:T(8,128)(2,1)}, bf16[1024,256]{1,0:T(8,128)(2,1)S(1)}, u32[]{:S(2)}) copy-start(bf16[1024,256]{1,0:T(8,128)(2,1)S(1)} %copy.140) | copy-start | bytes 1572868
  74.1 1.4 copy-start.3
  75.6 11.1 %copy-start.23 = (bf16[1024,256]{0,1:T(8,128)(2,1)S(1)}, bf16[1024,256]{0,1:T(8,128)(2,1)}, u32[]{:S(2)}) copy-start(bf16[1024,256]{0,1:T(8,128)(2,1)} %all_gather.17) | copy-start | bytes 1572868
  86.7 2.1 copy-start.14
  128.3 1.0 copy-start.5
  129.3 0.8 copy-start.16
  130.1 1.4 copy-start.18
  138.9 6.0 %copy-start.13 = (bf16[2,1,128,1024]{3,2,1,0:T(8,128)(2,1)S(1)}, bf16[2,1,128,1024]{3,2,1,0:T(8,128)(2,1)}, u32[]{:S(2)}) copy-start(bf16[2,1,128,1024]{3,2,1,0:T(8,128)(2,1)} %param.19) | copy-start | bytes 1572868
  138.9 6.0 %copy-start.17 = (bf16[2,128,1024]{2,1,0:T(8,128)(2,1)S(1)}, bf16[2,128,1024]{2,1,0:T(8,128)(2,1)}, u32[]{:S(2)}) copy-start(bf16[2,128,1024]{2,1,0:T(8,128)(2,1)} %copy-done.16) | copy-start | bytes 1572868
  144.9 41.2 %copy-start.28 = (bf16[1024,1024]{1,0:T(8,128)(2,1)S(1)}, bf16[1024,1024]{1,0:T(8,128)(2,1)}, u32[]{:S(2)}) copy-start(bf16[1024,1024]{1,0:T(8,128)(2,1)} %get-tuple-element.136) | copy-start | bytes 6291460
  185.1 1.0 copy-start.7
  191.4 6.8 %copy-start.19 = (bf16[2,4,128,1024]{3,2,1,0:T(8,128)(2,1)S(1)}, bf16[2,4,128,1024]{3,2,1,0:T(8,128)(2,1)}, u32[]{:S(2)}) copy-start(bf16[2,4,128,1024]{3,2,1,0:T(8,128)(2,1)} %copy-done.18) | copy-start | bytes 6291460
  198.2 3.8 copy-start.29
  205.7 6.1 %copy-start.6 = (f32[2,128,1024]{2,1,0:T(8,128)S(1)}, f32[2,128,1024]{2,1,0:T(8,128)}, u32[]{:S(2)}) copy-start(f32[2,128,1024]{2,1,0:T(8,128)} %copy-done.5) | copy-start | bytes 3145732
  205.7 6.1 %copy-start.8 = (f32[2,128,1024]{2,1,0:T(8,128)S(1)}, f32[2,128,1024]{2,1,0:T(8,128)}, u32[]{:S(2)}) copy-start(f32[2,128,1024]{2,1,0:T(8,128)} %copy-done.7) | copy-start | bytes 3145732
  211.8 39.2 %copy-start.15 = (bf16[2,512,256]{2,1,0:T(8,128)(2,1)S(1)}, bf16[2,512,256]{2,1,0:T(8,128)(2,1)}, u32[]{:S(2)}) copy-start(bf16[2,512,256]{2,1,0:T(8,128)(2,1)} %copy-done.14) | copy-start | bytes 1572868
  251.0 1.0 copy-start.1
  251.0 1.4 copy-start.24
  254.0 1.6 copy-start.10
  255.0 65.8 %reduce-scatter.11.cloned.1.call-start = ((), (), s32[]{:S(2)}) async-start(), calls=%async_computation.9 | async-start | bytes 2359296 | tf_op jit(solution)/shard_map/reduce_scatter | solution.py:435
  255.6 106.6 %reduce-scatter.5.cloned.1.call-start = ((), (), s32[]{:S(2)}) async-start(), calls=%async_computation.6 | async-start | bytes 3538944 | tf_op jit(solution)/shard_map/reduce_scatter | solution.py:460
  255.6 1.2 copy-start.4
  256.8 1.0 copy-start.20
  257.9 15.7 %copy-start.21 = (bf16[1152,768]{1,0:T(8,128)(2,1)S(1)}, bf16[1152,768]{1,0:T(8,128)(2,1)}, u32[]{:S(2)}) copy-start(bf16[1152,768]{1,0:T(8,128)(2,1)} %all-gather.9.cloned.1.call-done) | copy-start | bytes 5308420
  273.6 5.2 %copy-start.11 = (bf16[2,512,256]{2,1,0:T(8,128)(2,1)}, bf16[2,512,256]{2,1,0:T(8,128)(2,1)S(1)}, u32[]{:S(2)}) copy-start(bf16[2,512,256]{2,1,0:T(8,128)(2,1)S(1)} %get-tuple-element.45) | copy-start | bytes 1572868
  273.6 2.7 copy-start.22
  273.6 2.7 collective-permute-start.1
  276.6 2.2 copy-start.25
  276.6 2.2 copy-start.26
  281.0 3.8 copy-start.12
  288.3 111.7 %reduce-scatter.9.cloned.1.call-start = ((), (), s32[]{:S(2)}) async-start(), calls=%async_computation.8 | async-start | bytes 2654208 | tf_op jit(solution)/shard_map/reduce_scatter | solution.py:436
  289.1 1.2 copy-start.2
Sparse Core Ops, SparseCore 0:
  12.0 29.0 all-gather.8
  42.8 32.8 all-gather.4
  77.2 30.5 all-gather.6
  255.1 29.5 reduce-scatter.6
  286.9 33.8 reduce-scatter.10
  322.9 39.2 reduce-scatter.4
  364.5 35.4 reduce-scatter.8

commit v2 on v1

--- a/solution.py
+++ b/solution.py
@@ -42,12 +42,14 @@
     return jnp.sum(rows, 0, keepdims=True)
 
 
-def exchange_kernel(n, parts, has_sum, has_send, tail, work, n_in, n_out, *refs):
+def exchange_kernel(n, far, parts, has_sum, has_send, tail, work, n_in, n_out, n_grad, *refs):
     refs = list(refs)
     partial = refs.pop(0) if has_sum else None
     ins = [refs.pop(0) for _ in range(n_in)]
+    grads = [refs.pop(0) for _ in range(n_grad)]
     gathered = refs.pop(0) if has_send else None
     outs = [refs.pop(0) for _ in range(n_out)]
+    grad_outs = [refs.pop(0) for _ in range(n_grad)]
     relay = n == 4
     if has_sum:
         landing, sum_send, sum_recv = refs.pop(0), refs.pop(0), refs.pop(0)
@@ -57,24 +59,45 @@
         all_send, all_recv = refs.pop(0), refs.pop(0)
     if tail:
         tail_land, tail_send, tail_recv = refs.pop(0), refs.pop(0), refs.pop(0)
+    grad_scratch = [[refs.pop(0) for _ in range(6)] for _ in range(n_grad)]
     me = lax.axis_index("heads")
 
-    def start(src, dst, send_sem, recv_sem, k):
+    def start_at(src, dst, send_sem, recv_sem, target):
         copy = pltpu.make_async_remote_copy(
             src_ref=src,
             dst_ref=dst,
             send_sem=send_sem,
             recv_sem=recv_sem,
-            device_id={"heads": me ^ k},
+            device_id=target,
             device_id_type=MESH,
         )
         copy.start()
         return copy
 
+    def start(src, dst, send_sem, recv_sem, k):
+        return start_at(src, dst, send_sem, recv_sem, {"heads": me ^ k})
+
     barrier = pltpu.get_barrier_semaphore()
     for k in range(1, n):
         pl.semaphore_signal(barrier, inc=1, device_id={"heads": me ^ k}, device_id_type=MESH)
-    pl.semaphore_wait(barrier, n - 1)
+    if n_grad:
+        side = lax.axis_index("seq")
+        place = lax.axis_index("dp")
+        ahead = [lax.rem(place + j, far) for j in range(far)]
+        for target in [{"seq": 1 - side}] + [{"dp": ahead[j]} for j in range(1, far)]:
+            pl.semaphore_signal(barrier, inc=1, device_id=target, device_id_type=MESH)
+    pl.semaphore_wait(barrier, n - 1 + (far if n_grad else 0))
+
+    core_copies, far_copies = {}, {}
+    for at, (ref, scratch) in enumerate(zip(grads, grad_scratch)):
+        for j in list(range(1, far)) + [0]:
+            core_copies[at, j] = start_at(
+                ref.at[2 * ahead[j] + 1 - side],
+                scratch[0].at[ahead[j]],
+                scratch[2].at[j],
+                scratch[3].at[j],
+                {"seq": 1 - side},
+            )
 
     own = (partial if has_sum else gathered).shape[2]
     halves = (pl.ds(0, own // 2), pl.ds(own // 2, own // 2))
@@ -100,6 +123,20 @@
                     sum_recv.at[part, k - 1],
                     k,
                 )
+    for at, (ref, scratch) in enumerate(zip(grads, grad_scratch)):
+        for j in range(1, far):
+            core_copies[at, j].wait_recv()
+            scratch[0][ahead[j]] = (
+                ref[2 * ahead[j] + side].astype(F32) + scratch[0][ahead[j]].astype(F32)
+            ).astype(ref.dtype)
+            far_copies[at, j] = start_at(
+                scratch[0].at[ahead[j]],
+                scratch[1].at[j - 1],
+                scratch[4].at[j - 1],
+                scratch[5].at[j - 1],
+                {"dp": ahead[j]},
+            )
+    if has_sum and relay:
         for part in range(parts):
             for k in (1, 2):
                 other, half = 3 - k, halves[k - 1]
@@ -115,7 +152,7 @@
                     sum_recv.at[part, 1 + other],
                     other,
                 )
-    elif has_sum:
+    if has_sum and not relay:
         for part in range(parts):
             for k in range(1, n):
                 sums[part, k, 0] = start(
@@ -180,18 +217,28 @@
         outs[-1][...] = sum(tail_land[k, 0:6] for k in range(n))
         for copy in tails:
             copy.wait_send()
+    for at, (ref, scratch) in enumerate(zip(grads, grad_scratch)):
+        core_copies[at, 0].wait_recv()
+        total = ref[2 * place + side].astype(F32) + scratch[0][place].astype(F32)
+        for j in range(1, far):
+            far_copies[at, j].wait_recv()
+            total = total + scratch[1][j - 1].astype(F32)
+        grad_outs[at][...] = total
+    started += list(core_copies.values()) + list(far_copies.values())
     for copy in list(relays.values()) + list(sums.values()) + list(sends.values()) + started:
         copy.wait_send()
 
 
-def exchange(n, name, ident, work, partial, ins, out_shapes, has_send, shape, tail=False):
+def exchange(n, name, ident, work, partial, ins, out_shapes, has_send, shape, tail=False, grads=()):
     parts, rows, width = shape
     has_sum = partial is not None
     relay = n == 4
-    operands = ([partial] if has_sum else []) + list(ins)
+    far = lax.axis_size("dp")
+    operands = ([partial] if has_sum else []) + list(ins) + list(grads)
     shapes = ([jax.ShapeDtypeStruct((parts, n, rows, width), BF16)] if has_send else []) + [
         jax.ShapeDtypeStruct(s, t) for s, t in out_shapes
     ]
+    shapes += [jax.ShapeDtypeStruct(g.shape[1:], F32) for g in grads]
     sems = pltpu.SemaphoreType.DMA((parts, 4 if relay else n - 1))
     scratch = []
     if has_sum:
@@ -203,9 +250,13 @@
         scratch += [sems, sems]
     if tail:
         scratch += [pltpu.VMEM((n, 8, width), F32)] + [pltpu.SemaphoreType.DMA((n - 1,))] * 2
+    for g in grads:
+        scratch += [pltpu.VMEM((count,) + g.shape[1:], g.dtype) for count in (far, far - 1)]
+        scratch += [pltpu.SemaphoreType.DMA((far,))] * 2 + [pltpu.SemaphoreType.DMA((far - 1,))] * 2
     return pl.pallas_call(
         functools.partial(
-            exchange_kernel, n, parts, has_sum, has_send, tail, work, len(ins), len(out_shapes)
+            exchange_kernel, n, far, parts, has_sum, has_send, tail, work, len(ins),
+            len(out_shapes), len(grads),
         ),
         out_shape=shapes,
         in_specs=[VMEM_SPEC] * len(operands),
@@ -367,20 +418,21 @@
     piece = (micro, own, width)
 
     small = jnp.concatenate([v.reshape(-1) for v in (b_qv, b_up, ln_gains, ln_shifts)])
-    small_rows = -(-small.size // (3 * cols * 16)) * 16
-    small = jnp.pad(small, (0, small_rows * 3 * cols - small.size)).reshape(small_rows, 3 * cols)
-    qkv_mine = jnp.concatenate([jnp.swapaxes(w_qkv, 0, 1).reshape(depth, 3 * cols), small], 0)
-    qkv_all = lax.all_gather(qkv_mine, share, axis=0, tiled=False)
+    small = jnp.pad(small, (0, -small.size % (16 * 4 * cols))).reshape(-1, 4 * cols)
+    attn_mine = jnp.concatenate([w_qkv[0], w_qkv[1], w_qkv[2], w_out.T], 1)
+    attn_all = lax.all_gather(jnp.concatenate([attn_mine, small], 0), share, axis=0, tiled=False)
     x_rows = inputs[:, 0]
     (gathered,) = exchange(n, "gather_inputs", 0, work_inputs, None, [x_rows], [], True, piece)
     gathered = gathered.reshape(micro * rows, width)
-    out_all = lax.all_gather(w_out.T, share, axis=0, tiled=True)
     up_all = lax.all_gather(w_up, share, axis=0, tiled=True)
     down_all = lax.all_gather(w_down.T, share, axis=0, tiled=True)
 
-    q_weights = qkv_all[:, :depth, :cols].reshape(owners * depth, cols)
-    kv_weights = qkv_all[:, :depth, cols:].reshape(owners * depth, 2 * cols)
-    small_all = qkv_all[:, depth:].reshape(owners, -1)
+    attn_weights = attn_all[:, :depth].reshape(owners * depth, 4 * cols)
+    q_weights = attn_weights[:, :cols]
+    kv_weights = attn_weights[:, cols : 3 * cols]
+    qkv_weights = attn_weights[:, : 3 * cols]
+    out_all = attn_weights[:, 3 * cols :]
+    small_all = attn_all[:, depth:].reshape(owners, -1)
     at = 0
     pieces = []
     for v in (b_qv, b_up, ln_gains, ln_shifts):
@@ -419,65 +471,58 @@
     d_pre_wide = dot(d_mlp, down_all, NN) * slope
     d_pre = d_pre_wide.astype(BF16)
     partial = dot(d_pre, up_all, NT).astype(BF16).reshape(micro, n, own, width)
-    g_down = dot(d_mlp, hidden, TN).astype(BF16)
-    g_up = dot(normed_all, d_pre, TN).astype(BF16)
+    def owned(wide):
+        return wide.astype(BF16).reshape(owners, -1, wide.shape[-1])
+
+    def owned_small(values):
+        return jnp.pad(values, ((0, 0), (0, -values.shape[-1] % 1024))).reshape(owners, 8, -1)
+
+    g_down = owned(dot(d_mlp, hidden, TN))
+    g_up = owned(dot(normed_all, d_pre, TN))
     g_bup = jnp.sum(d_pre.astype(F32), 0).reshape(b_up.shape[0], owners, b_up.shape[1])
-    g_bup = jnp.swapaxes(g_bup, 0, 1).reshape(owners, -1)
-
-    def with_extra(wide, extra):
-        wide = wide.reshape(owners, -1, wide.shape[-1])
-        span = wide.shape[-1]
-        extra = jnp.pad(extra, ((0, 0), (0, -extra.shape[-1] % (16 * span)))).astype(BF16)
-        return jnp.concatenate([wide, extra.reshape(owners, -1, span)], 1)
-
-    g_up = with_extra(g_up, g_bup)
-    partial, g_down, g_up = lax.optimization_barrier((partial, g_down, g_up))
-    g_down = lax.psum_scatter(g_down, share, scatter_dimension=0, tiled=True)
-    g_up = lax.psum_scatter(g_up, share, scatter_dimension=0, tiled=False)
-    d_attn, d_first, _, norm_sums = exchange(
+    g_bup = owned_small(jnp.swapaxes(g_bup, 0, 1).reshape(owners, -1))
+    d_attn, d_first, _, norm_sums, g_down, g_up, g_bup = exchange(
         n, "first_norm_back", 3, work_third, partial, [first, d_second, gains, sums_two],
         [(piece, F32), ((micro, 3, width), F32), ((6, width), F32)], True, piece, tail=True,
+        grads=[g_down, g_up, g_bup],
     )
 
     d_attn = d_attn.reshape(micro * rows, width)
     d_mixed = dot(d_attn, out_all, NN).astype(BF16).reshape(micro, rows, cols)
     norm_sums = jnp.swapaxes(norm_sums.reshape(6, owners, depth), 0, 1).reshape(owners, -1)
-    g_out = with_extra(dot(d_attn, mixed_rows, TN).astype(BF16), norm_sums)
-    d_mixed, g_out = lax.optimization_barrier((d_mixed, g_out))
-    g_out = lax.psum_scatter(g_out, share, scatter_dimension=0, tiled=False)
+    g_out = owned(dot(d_attn, mixed_rows, TN))
     d_query, d_kv, d_far = attention_call(
         attend_back_kernel, "attend_back", queries, kv, kv_far, [d_mixed], [logs],
         ["row", "pair", "far"], 5, head,
     )
     d_kv = (d_kv + lax.ppermute(d_far, "seq", swap).astype(F32)).astype(BF16)
     d_qkv = jnp.concatenate([d_query, d_kv[0], d_kv[1]], -1).reshape(micro * rows, 3 * cols)
-    qkv_weights = qkv_all[:, :depth].reshape(owners * depth, 3 * cols)
     partial = dot(d_qkv, qkv_weights, NT).astype(BF16).reshape(micro, n, own, width)
     sums = jnp.sum(d_qkv.astype(F32), 0).reshape(3, heads_here, owners, head // owners)
     g_bqv = jnp.moveaxis(jnp.stack([sums[0], sums[2]]), 2, 0).reshape(owners, -1)
-    g_qkv = with_extra(dot(gathered, d_qkv, TN).astype(BF16), g_bqv)
-    partial, g_qkv = lax.optimization_barrier((partial, g_qkv))
-    g_qkv = lax.psum_scatter(g_qkv, share, scatter_dimension=0, tiled=False)
-    (d_inputs,) = exchange(
-        n, "input_grad", 4, work_last, partial, [d_first], [(piece, BF16)], False, piece
-    )
-
-    norm_mine = g_out[depth:].reshape(-1)[: 6 * depth].astype(F32).reshape(6, depth)
+    g_small = owned_small(jnp.concatenate([g_bqv, norm_sums], 1))
+    g_qkv = owned(dot(gathered, d_qkv, TN))
+    d_inputs, g_out, g_qkv, g_small = exchange(
+        n, "input_grad", 4, work_last, partial, [d_first], [(piece, BF16)], False, piece,
+        grads=[g_out, g_qkv, g_small],
+    )
+
+    g_small = g_small.reshape(-1)
+    bqv_grad = g_small[: b_qv.size].reshape(b_qv.shape)
+    norm_mine = g_small[b_qv.size : b_qv.size + 6 * depth].reshape(6, depth)
     gain_grad = jnp.stack([norm_mine[0], norm_mine[3]])
     shift_grad = jnp.stack([norm_mine[1], norm_mine[2], norm_mine[4], norm_mine[5]])
-    qkv_grad = jnp.swapaxes(g_qkv[:depth].astype(F32).reshape(depth, 3, cols), 0, 1)
-    bqv_grad = g_qkv[depth:].reshape(-1)[: b_qv.size].astype(F32).reshape(b_qv.shape)
-    up_grad = g_up[:depth].astype(F32)
-    bup_grad = g_up[depth:].reshape(-1)[: b_up.size].astype(F32).reshape(b_up.shape)
+    qkv_grad = jnp.swapaxes(g_qkv.reshape(depth, 3, cols), 0, 1)
+    bup_grad = g_bup.reshape(-1)[: b_up.size].reshape(b_up.shape)
     return (
         result[:, None],
         d_inputs[:, None],
         qkv_grad,
         bqv_grad,
-        g_out[:depth].astype(F32).T,
-        up_grad,
+        g_out.T,
+        g_up,
         bup_grad,
-        g_down.astype(F32).T,
+        g_down.T,
         gain_grad,
         shift_grad,
     )

time: 417 us -> 327 us (0.78)
  waiting for transfers between devices: 89.1 us -> 12.4 us
  Pallas kernels: 188 us -> 212 us
  blocking collectives: 18.8 us -> 0 us
  other arithmetic: 14.9 us -> 4.86 us
  local copies, waits for them, and re-layouts: 35.5 us -> 28.8 us
    reduce_scatter x4 -> x0, waiting for transfers between devices: 79.4 us -> none  [the longest x1 39.4 us: local(): g_qkv = lax.psum_scatter(g_qkv, share, scatter_dimension=0, tiled=False)]
    pallas_call x5, Pallas kernels: 162 us -> 186 us  [exchange(): pl.pallas_call(functools.partial(exchange_kernel, n, far, parts, has_sum,...]
    all_gather x1 -> x0, blocking collectives: 18.8 us -> none  [local(): out_all = lax.all_gather(w_out.T, share, axis=0, tiled=True)]
    concatenate x4 -> x1, other arithmetic: 7.97 us -> 0.75 us  [local(): jnp.concatenate([attn_mine, small], 0)]
    slice x10 -> x4, local copies, waits for them, and re-layouts: 9.3 us -> 3.87 us  [the longest x1 3.14 us: local(): attn_weights = attn_all[:, :depth].reshape(owners * depth, 4 * cols)]
    all_gather x1, waiting for transfers between devices: 5.76 us -> 11 us  [local(): lax.all_gather(jnp.concatenate([attn_mine, small], 0), share, axis=0, til...]
    unnamed x75 -> x77, local copies, waits for them, and re-layouts: 17.6 us -> 16.4 us
  transfers between devices with their start and end apart: 9 -> 5, of which waited for: 5 -> 1; matrix products, arithmetic and copies ran while one was open for 11% -> 10% of each run, Pallas kernels for 26% -> 22%
where the time goes in v2:
time: 327 us; the launch traced here: 326 us
  Pallas kernels  212 us (65%)
  matrix products  53.3 us (16%)
  local copies, waits for them, and re-layouts  28.8 us (9%)
  between operations  14.3 us (4%)
  waiting for transfers between devices  12.4 us (4%)
  other arithmetic  4.86 us (1%)
    pallas_call x5, Pallas kernels, exchange(): pl.pallas_call(functools.partial(exchange_kernel, n, far, parts, has_sum,...  186 us
    dot_general x13, matrix products, dot(): lax.dot_general(left, right, (dims, ((), ())), preferred_element_type=F32)  53.3 us
    pallas_call x2, Pallas kernels, attention_call(): pl.pallas_call(functools.partial(kernel, head), grid=(micro, blocks), in_...  26.4 us
    unnamed x77, local copies, waits for them, and re-layouts  16.4 us
    all_gather x1, waiting for transfers between devices, local(): lax.all_gather(jnp.concatenate([attn_mine, small], 0), share, axis=0, til...  11 us
  transfers between devices with their start and end apart: 5, of which 1 were waited for; matrix products, arithmetic and copies ran while one was open for 10% of the time, Pallas kernels for 22%

profile of v2, /device:TPU:0, one launch (start us, length us, event | category | flops | bytes accessed | tf_op | source)
XLA Modules:
  0.0 326.2 jit_solution(4625561279965211995)
XLA Ops:
  7.2 0.8 reshape.195
  8.0 0.8 copy.49
  8.9 0.8 fusion.21
  9.7 0.9 copy.48
  10.6 0.9 slice_bitcast_fusion.3
  11.6 0.7 pad_maximum_fusion.1
  12.4 0.7 all-gather.5.cloned.1.call-update
  13.1 0.7 all-gather.7.cloned.1.call-update
  13.8 21.9 %gather_inputs.1 = bf16[2,4,128,1024]{3,2,1,0:T(8,128)(2,1)S(1)} custom-call(bf16[2,128,1024]{2,1,0:T(8,128)(2,1)S(1)} %bitcast.138), custom_call_target="tpu_custom_call" | custom-call | flops 1000000 | bytes 60000000 | tf_op jit(solution)/shard_map/gather_inputs/pallas_call | solution.py:256
  35.8 11.0 %all-gather.9.cloned.1.call-done = bf16[1152,1024]{1,0:T(8,128)(2,1)} async-done(((bf16[144,1024]{1,0:T(8,128)(2,1)}), bf16[1152,1024]{1,0:T(8,128)(2,1)}) %all-gather.9.cloned.1.call-update) | async-done | bytes 2359312 | tf_op jit(solution)/shard_map/all_gather | solution.py:423
  46.8 3.1 slice.172
  50.0 1.0 slice_bitcast_fusion
  51.3 3.5 %fusion.8 = bf16[1024,512]{0,1:T(8,128)(2,1)} fusion(bf16[1024,1024]{1,0:T(8,128)(2,1)S(1)} %bitcast.140, bf16[1024,1024]{1,0:T(8,128)(2,1)} %bitcast.176, f32[512]{0:T(512)S(1)} %concatenate.28), kind=kOutput, calls=%fused_computation.23 | convolution fusion | flops 1074790400 | bytes 4196352 | tf_op jit(solution)/shard_map/dot_general | solution.py:19
  54.8 2.4 copy.52
  57.9 2.6 fusion.10
  60.5 1.2 copy.51
  61.8 1.2 copy-done.7
  63.0 11.1 %attend.1 = (bf16[2,512,256]{2,1,0:T(8,128)(2,1)S(1)}, f32[2,2,2,512]{3,2,1,0:T(2,128)S(1)}) custom-call(bf16[2,512,256]{2,1,0:T(8,128)(2,1)S(1)} %bitcast.153, bf16[2,512,512]{2,1,0:T(8,128)(2,1)S(1)} %bitcast.144, bf16[2,512,512]{2,1,0:T(8,128)(2,1)S(1)} %bitcast.145, bf16[2,512,512]{2,1,0:T(8,128)(2,1)} %collective-permute-done.k_far.v_far, ...), custom_call_target="tpu_custom_call" | custom-call | flops 4294967296 | bytes 20000000 | tf_op jit(solution)/shard_map/attend/pallas_call | solution.py:386
  74.1 3.3 %convolution_convert_fusion.4 = bf16[1024,1024]{1,0:T(8,128)(2,1)} fusion(bf16[1024,256]{1,0:T(8,128)(2,1)S(1)} %bitcast.158, bf16[1024,1024]{1,0:T(8,128)(2,1)} %bitcast.178), kind=kOutput, calls=%fused_computation.17 | convolution fusion | flops 537919488 | bytes 3145728 | tf_op jit(solution)/shard_map/dot_general | solution.py:19
  77.4 39.5 %first_norm.1 = (bf16[2,4,128,1024]{3,2,1,0:T(8,128)(2,1)S(1)}, f32[2,128,1024]{2,1,0:T(8,128)S(1)}, bf16[2,128,1024]{2,1,0:T(8,128)(2,1)S(1)}) custom-call(bf16[2,4,128,1024]{3,2,1,0:T(8,128)(2,1)} %bitcast.175, bf16[2,128,1024]{2,1,0:T(8,128)(2,1)S(1)} %bitcast.139, f32[2,1024]{1,0:T(2,128)S(1)} %bitcast.162, f32[4,1024]{1,0:T(4,128)S(1)} %bitcast.160), custom_call_target="tpu_custom_call" | custom-call | flops 1000000 | bytes 60000000 | tf_op jit(solution)/shard_map/first_norm/pallas_call | solution.py:256
  116.9 1.0 copy-done.3
  117.9 0.8 copy-done.19
  118.7 1.3 copy-done.22
  120.0 7.4 %multiply_convert_fusion = (bf16[1024,1024]{1,0:T(8,128)(2,1)}, f32[1024,1024]{1,0:T(8,128)}) fusion(f32[1024]{0:T(1024)S(1)} %reshape.230, bf16[1024,1024]{1,0:T(8,128)(2,1)} %bitcast.170, bf16[1024,1024]{1,0:T(8,128)(2,1)} %all-gather.5.cloned.1.call-done), kind=kOutput, calls=%fused_computation.8 | convolution fusion | flops 2153775104 | bytes 10489856 | tf_op jit(solution)/shard_map/dot_general | solution.py:19
  127.4 5.9 %convolution_convert_fusion.3 = bf16[1024,1024]{1,0:T(8,128)(2,1)} fusion(bf16[1024,1024]{1,0:T(8,128)(2,1)} %get-tuple-element.99, bf16[1024,1024]{0,1:T(8,128)(2,1)} %all-gather.7.cloned.1.call-done), kind=kOutput, calls=%fused_computation.16 | convolution fusion | flops 2148532224 | bytes 6291456 | tf_op jit(solution)/shard_map/dot_general | solution.py:19
  133.4 38.8 %second_norm.1 = (bf16[2,4,128,1024]{3,2,1,0:T(8,128)(2,1)S(1)}, bf16[2,128,1024]{2,1,0:T(8,128)(2,1)S(1)}, f32[2,128,1024]{2,1,0:T(8,128)S(1)}, f32[2,3,1024]{2,1,0:T(4,128)S(1)}) custom-call(bf16[2,4,128,1024]{3,2,1,0:T(8,128)(2,1)} %bitcast.186, bf16[2,128,1024]{2,1,0:T(8,128)(2,1)S(1)} %copy-done.20, bf16[2,128,1024]{2,1,0:T(8,128)(2,1)S(1)} %bitcast.157, ...), custom_call_target="tpu_custom_call" | custom-call | flops 1000000 | bytes 60000000 | tf_op jit(solution)/shard_map/second_norm/pallas_call | solution.py:256
  172.2 3.8 %convolution_convert_fusion.1 = bf16[1024,1024]{1,0:T(8,128)(2,1)} fusion(bf16[1024,1024]{1,0:T(8,128)(2,1)S(1)} %bitcast.172, bf16[1024,1024]{1,0:T(8,128)(2,1)S(1)} %copy-done.28), kind=kOutput, calls=%fused_computation.14 | convolution fusion | flops 2148532224 | bytes 6291456 | tf_op jit(solution)/shard_map/dot_general | solution.py:19
  176.1 4.2 %convert_reduce_fusion = (f32[1024]{0:T(1024)S(1)}, bf16[1024,1024]{1,0:T(8,128)(2,1)S(1)}) fusion(f32[1024,1024]{1,0:T(8,128)S(1)} %copy-done.27, f32[1024]{0:T(1024)S(1)} %reshape.230, bf16[1024,1024]{1,0:T(8,128)(2,1)S(1)} %bitcast.173, bf16[1024,1024]{0,1:T(8,128)(2,1)S(1)} %copy-done.26), kind=kOutput, calls=%fused_computation.7 | convolution fusion | flops 2161114112 | bytes 10493952 | tf_op jit(solution)/shard_map/dot_general | solution.py:19
  180.2 3.8 %convolution_convert_fusion = bf16[1024,1024]{1,0:T(8,128)(2,1)} fusion(bf16[1024,1024]{1,0:T(8,128)(2,1)S(1)} %bitcast.171, bf16[1024,1024]{1,0:T(8,128)(2,1)S(1)} %get-tuple-element.102), kind=kOutput, calls=%fused_computation.13 | convolution fusion | flops 2148532224 | bytes 6291456 | tf_op jit(solution)/shard_map/dot_general | solution.py:19
  184.3 6.1 %convolution_convert_fusion.2 = bf16[1024,1024]{1,0:T(8,128)(2,1)} fusion(bf16[1024,1024]{1,0:T(8,128)(2,1)} %copy-done.29, bf16[1024,1024]{1,0:T(8,128)(2,1)} %all-gather.5.cloned.1.call-done), kind=kOutput, calls=%fused_computation.15 | convolution fusion | flops 2148532224 | bytes 6291456 | tf_op jit(solution)/shard_map/dot_general | solution.py:19
  190.4 55.0 %first_norm_back.1 = (bf16[2,4,128,1024]{3,2,1,0:T(8,128)(2,1)}, f32[2,128,1024]{2,1,0:T(8,128)S(1)}, f32[2,3,1024]{2,1,0:T(4,128)}, f32[6,1024]{1,0:T(8,128)S(1...) custom-call(bf16[2,4,128,1024]{3,2,1,0:T(8,128)(2,1)} %bitcast.185, ...), custom_call_target="tpu_custom_call" | custom-call | flops 1000000 | bytes 60000000 | tf_op jit(solution)/shard_map/first_norm_back/pallas_call | solution.py:256
  245.4 3.1 convolution_convert_fusion.8
  248.6 15.3 %attend_back.1 = (bf16[2,512,256]{2,1,0:T(8,128)(2,1)S(1)}, f32[2,2,512,256]{3,2,1,0:T(8,128)}, bf16[2,2,512,256]{3,2,1,0:T(8,128)(2,1)}) custom-call(bf16[2,512,256]{2,1,0:T(8,128)(2,1)S(1)} %bitcast.154, bf16[2,512,512]{2,1,0:T(8,128)(2,1)S(1)} %bitcast.146, bf16[2,512,512]{2,1,0:T(8,128)(2,1)S(1)} %bitcast.147, ...), custom_call_target="tpu_custom_call" | custom-call | flops 10737418240 | bytes 20000000 | tf_op jit(solution)/shard_map/attend_back/pallas_call | solution.py:386
  264.3 0.7 copy.62
  265.0 2.0 copy.63
  267.0 3.4 %convolution_convert_fusion.7 = bf16[1024,256]{1,0:T(8,128)(2,1)} fusion(bf16[1024,1024]{1,0:T(8,128)(2,1)} %bitcast.208, bf16[1024,256]{1,0:T(8,128)(2,1)} %bitcast.159), kind=kOutput, calls=%fused_computation.25 | convolution fusion | flops 537133056 | bytes 3145728 | tf_op jit(solution)/shard_map/dot_general | solution.py:19
  270.4 1.6 add_convert_fusion
  272.1 3.0 fusion.7
  275.1 3.2 convolution_convert_fusion.5
  278.6 1.8 copy.55
  280.9 30.2 %input_grad.1 = (bf16[2,128,1024]{2,1,0:T(8,128)(2,1)S(1)}, f32[128,256]{1,0:T(8,128)S(1)}, f32[128,768]{1,0:T(8,128)S(1)}, f32[8,128]{1,0:T(8,128)S(1)}) custom-call(bf16[2,4,128,1024]{3,2,1,0:T(8,128)(2,1)} %bitcast.187, f32[2,128,1024]{2,1,0:T(8,128)S(1)} %copy-done.2, bf16[8,128,256]{2,1,0:T(8,128)(2,1)S(1)} %bitcast.148, ...), custom_call_target="tpu_custom_call" | custom-call | flops 1000000 | bytes 60000000 | tf_op jit(solution)/shard_map/input_grad/pallas_call | solution.py:256
  311.1 0.8 copy-done.15
  311.9 0.7 copy-done.21
  313.3 1.7 copy.61
  315.2 0.9 copy.60
  317.2 0.8 copy.85
  318.0 0.8 copy.86
  318.8 0.8 copy.87
  (106 shorter events, 4.8 us)
Async XLA Ops:
  7.2 6.7 %copy-start = (bf16[2,1,128,1024]{3,2,1,0:T(8,128)(2,1)S(1)}, bf16[2,1,128,1024]{3,2,1,0:T(8,128)(2,1)}, u32[]{:S(2)}) copy-start(bf16[2,1,128,1024]{3,2,1,0:T(8,128)(2,1)} %param.10) | copy-start | bytes 1572868
  7.2 39.6 %all-gather.9.cloned.1.call-start = ((), (), s32[]{:S(2)}) async-start(), calls=%async_computation.2 | async-start | bytes 2654208 | tf_op jit(solution)/shard_map/all_gather | solution.py:423
  12.3 107.7 %all-gather.5.cloned.1.call-start = ((), (), s32[]{:S(2)}) async-start(), calls=%async_computation | async-start | bytes 2359296 | tf_op jit(solution)/shard_map/all_gather | solution.py:427
  13.1 114.3 %all-gather.7.cloned.1.call-start = ((), (), s32[]{:S(2)}) async-start(), calls=%async_computation.1 | async-start | bytes 2359296 | tf_op jit(solution)/shard_map/all_gather | solution.py:428
  57.2 4.5 %collective-permute-start = (bf16[2,512,512]{2,1,0:T(8,128)(2,1)}, bf16[2,512,512]{2,1,0:T(8,128)(2,1)}, u32[]{:S(2)}, u32[]{:S(2)}) collective-permute-start(bf16[2,512,512]{2,1,0:T(8,128)(2,1)} %bitcast.143), channel_id=1, source_target_pairs={{0,4},{4,0},{1,5},{5,1},{2,6},{6,2},{3,7},{7,3},{8,12},{12,8},{9,1... | collective-permute-start | bytes 3145736 | tf_op jit(solution)/shard_map/ppermute | solution.py:448
  61.7 1.2 copy-start.7
  74.1 3.3 %copy-start.18 = (bf16[2,512,256]{2,1,0:T(8,128)(2,1)}, bf16[2,512,256]{2,1,0:T(8,128)(2,1)S(1)}, u32[]{:S(2)}) copy-start(bf16[2,512,256]{2,1,0:T(8,128)(2,1)S(1)} %get-tuple-element.32) | copy-start | bytes 1572868
  116.9 1.0 copy-start.3
  117.9 0.8 copy-start.19
  118.7 1.3 copy-start.22
  127.4 5.9 %copy-start.17 = (bf16[2,1,128,1024]{3,2,1,0:T(8,128)(2,1)S(1)}, bf16[2,1,128,1024]{3,2,1,0:T(8,128)(2,1)}, u32[]{:S(2)}) copy-start(bf16[2,1,128,1024]{3,2,1,0:T(8,128)(2,1)} %param.19) | copy-start | bytes 1572868
  127.4 5.9 %copy-start.20 = (bf16[2,128,1024]{2,1,0:T(8,128)(2,1)S(1)}, bf16[2,128,1024]{2,1,0:T(8,128)(2,1)}, u32[]{:S(2)}) copy-start(bf16[2,128,1024]{2,1,0:T(8,128)(2,1)} %copy-done.19) | copy-start | bytes 1572868
  133.4 38.9 %copy-start.28 = (bf16[1024,1024]{1,0:T(8,128)(2,1)S(1)}, bf16[1024,1024]{1,0:T(8,128)(2,1)}, u32[]{:S(2)}) copy-start(bf16[1024,1024]{1,0:T(8,128)(2,1)} %get-tuple-element.99) | copy-start | bytes 6291460
  172.2 3.8 %copy-start.5 = (f32[2,128,1024]{2,1,0:T(8,128)}, f32[2,128,1024]{2,1,0:T(8,128)S(1)}, u32[]{:S(2)}) copy-start(f32[2,128,1024]{2,1,0:T(8,128)S(1)} %get-tuple-element.38.refs_2_) | copy-start | bytes 3145732
  172.2 3.8 %copy-start.10 = (bf16[2,128,1024]{2,1,0:T(8,128)(2,1)}, bf16[2,128,1024]{2,1,0:T(8,128)(2,1)S(1)}, u32[]{:S(2)}) copy-start(bf16[2,128,1024]{2,1,0:T(8,128)(2,1)S(1)} %get-tuple-element.35) | copy-start | bytes 1572868
  172.2 3.8 %copy-start.26 = (bf16[1024,1024]{0,1:T(8,128)(2,1)S(1)}, bf16[1024,1024]{0,1:T(8,128)(2,1)}, u32[]{:S(2)}) copy-start(bf16[1024,1024]{0,1:T(8,128)(2,1)} %all-gather.7.cloned.1.call-done) | copy-start | bytes 6291460
  172.2 3.8 %copy-start.27 = (f32[1024,1024]{1,0:T(8,128)S(1)}, f32[1024,1024]{1,0:T(8,128)}, u32[]{:S(2)}) copy-start(f32[1024,1024]{1,0:T(8,128)} %get-tuple-element.100) | copy-start | bytes 12582916
  176.0 4.2 %copy-start.23 = (bf16[2,4,128,1024]{3,2,1,0:T(8,128)(2,1)S(1)}, bf16[2,4,128,1024]{3,2,1,0:T(8,128)(2,1)}, u32[]{:S(2)}) copy-start(bf16[2,4,128,1024]{3,2,1,0:T(8,128)(2,1)} %copy-done.22) | copy-start | bytes 6291460
  180.2 3.8 %copy-start.29 = (bf16[1024,1024]{1,0:T(8,128)(2,1)}, bf16[1024,1024]{1,0:T(8,128)(2,1)S(1)}, u32[]{:S(2)}) copy-start(bf16[1024,1024]{1,0:T(8,128)(2,1)S(1)} %get-tuple-element.102) | copy-start | bytes 6291460
  184.3 6.1 %copy-start.4 = (f32[2,128,1024]{2,1,0:T(8,128)S(1)}, f32[2,128,1024]{2,1,0:T(8,128)}, u32[]{:S(2)}) copy-start(f32[2,128,1024]{2,1,0:T(8,128)} %copy-done.3) | copy-start | bytes 3145732
  184.3 6.1 %copy-start.6 = (f32[2,128,1024]{2,1,0:T(8,128)S(1)}, f32[2,128,1024]{2,1,0:T(8,128)}, u32[]{:S(2)}) copy-start(f32[2,128,1024]{2,1,0:T(8,128)} %copy-done.5) | copy-start | bytes 3145732
  245.4 3.2 copy-start.1
  245.4 3.2 copy-start.12
  245.4 3.2 copy-start.14
  245.4 3.2 copy-start.8
  263.9 6.5 %collective-permute-start.1 = (bf16[2,2,512,256]{3,2,1,0:T(8,128)(2,1)}, bf16[2,2,512,256]{3,2,1,0:T(8,128)(2,1)}, u32[]{:S(2)}, u32[]{:S(2)}) collective-permute-start(bf16[2,2,512,256]{3,2,1,0:T(8,128)(2,1)} %get-tuple-element.44), channel_id=1, source_target_pairs={{0,4},{4,0},{1,5},{5,1},{2,6},{6,2},{3,7},{7,3},{8,12},{12,8},{9,1... | collective-permute-start | bytes 3145736 | tf_op jit(solution)/shard_map/ppermute | solution.py:498
  267.0 3.4 %copy-start.25 = (f32[2,2,512,256]{3,2,1,0:T(8,128)S(1)}, f32[2,2,512,256]{3,2,1,0:T(8,128)}, u32[]{:S(2)}) copy-start(f32[2,2,512,256]{3,2,1,0:T(8,128)} %get-tuple-element.43) | copy-start | bytes 6291460
  272.1 3.0 copy-start.24
  278.6 2.3 copy-start.2
  278.6 2.3 copy-start.9
  311.1 0.8 copy-start.15
  311.9 0.7 copy-start.21
  312.5 4.7 %copy-start.11 = (bf16[2,128,1024]{2,1,0:T(8,128)(2,1)S(1)}, bf16[2,128,1024]{2,1,0:T(8,128)(2,1)}, u32[]{:S(2)}) copy-start(bf16[2,128,1024]{2,1,0:T(8,128)(2,1)} %copy-done.10) | copy-start | bytes 1572868
  312.5 6.3 %copy-start.13 = (f32[128,1024]{1,0:T(8,128)S(1)}, f32[128,1024]{1,0:T(8,128)}, u32[]{:S(2)}) copy-start(f32[128,1024]{1,0:T(8,128)} %copy-done.12) | copy-start | bytes 1572868
  312.5 5.5 %copy-start.16 = (bf16[2,128,1024]{2,1,0:T(8,128)(2,1)S(1)}, bf16[2,128,1024]{2,1,0:T(8,128)(2,1)}, u32[]{:S(2)}) copy-start(bf16[2,128,1024]{2,1,0:T(8,128)(2,1)} %copy-done.15) | copy-start | bytes 1572868
Sparse Core Ops, SparseCore 0:
  12.5 34.3 all-gather.8
  48.4 28.2 all-gather.4
  78.3 30.3 all-gather.6

commit v3 on v2

--- a/solution.py
+++ b/solution.py
@@ -42,14 +42,16 @@
     return jnp.sum(rows, 0, keepdims=True)
 
 
-def exchange_kernel(n, far, parts, has_sum, has_send, tail, work, n_in, n_out, n_grad, *refs):
+def exchange_kernel(n, far, parts, has_sum, has_send, tail, work, n_in, n_out, n_grad, n_spread, *refs):
     refs = list(refs)
     partial = refs.pop(0) if has_sum else None
     ins = [refs.pop(0) for _ in range(n_in)]
     grads = [refs.pop(0) for _ in range(n_grad)]
+    spread = [refs.pop(0) for _ in range(n_spread)]
     gathered = refs.pop(0) if has_send else None
     outs = [refs.pop(0) for _ in range(n_out)]
     grad_outs = [refs.pop(0) for _ in range(n_grad)]
+    spread_outs = [refs.pop(0) for _ in range(n_spread)]
     relay = n == 4
     if has_sum:
         landing, sum_send, sum_recv = refs.pop(0), refs.pop(0), refs.pop(0)
@@ -60,6 +62,7 @@
     if tail:
         tail_land, tail_send, tail_recv = refs.pop(0), refs.pop(0), refs.pop(0)
     grad_scratch = [[refs.pop(0) for _ in range(6)] for _ in range(n_grad)]
+    spread_sems = [[refs.pop(0), refs.pop(0)] for _ in range(n_spread)]
     me = lax.axis_index("heads")
 
     def start_at(src, dst, send_sem, recv_sem, target):
@@ -80,13 +83,31 @@
     barrier = pltpu.get_barrier_semaphore()
     for k in range(1, n):
         pl.semaphore_signal(barrier, inc=1, device_id={"heads": me ^ k}, device_id_type=MESH)
+    side = lax.axis_index("seq")
+    place = lax.axis_index("dp")
+    ahead = [lax.rem(place + j, far) for j in range(far)]
+    owners = []
     if n_grad:
-        side = lax.axis_index("seq")
-        place = lax.axis_index("dp")
-        ahead = [lax.rem(place + j, far) for j in range(far)]
-        for target in [{"seq": 1 - side}] + [{"dp": ahead[j]} for j in range(1, far)]:
-            pl.semaphore_signal(barrier, inc=1, device_id=target, device_id_type=MESH)
-    pl.semaphore_wait(barrier, n - 1 + (far if n_grad else 0))
+        owners = [{"seq": 1 - side}] + [{"dp": ahead[j]} for j in range(1, far)]
+    if n_spread:
+        owners = [
+            {"dp": ahead[j], "seq": 1 - side if c else side}
+            for j in range(far)
+            for c in (0, 1)
+            if j or c
+        ]
+    for target in owners:
+        pl.semaphore_signal(barrier, inc=1, device_id=target, device_id_type=MESH)
+    pl.semaphore_wait(barrier, n - 1 + len(owners))
+
+    spread_copies = []
+    mine = 2 * place + side
+    for src, dst, sems in zip(spread, spread_outs, spread_sems):
+        for at, target in enumerate(owners):
+            spread_copies.append(
+                start_at(src.at[...], dst.at[mine], sems[0].at[at], sems[1].at[at], target)
+            )
+        dst[mine] = src[...]
 
     core_copies, far_copies = {}, {}
     for at, (ref, scratch) in enumerate(zip(grads, grad_scratch)):
@@ -224,21 +245,24 @@
             far_copies[at, j].wait_recv()
             total = total + scratch[1][j - 1].astype(F32)
         grad_outs[at][...] = total
+    for copy in spread_copies:
+        copy.wait()
     started += list(core_copies.values()) + list(far_copies.values())
     for copy in list(relays.values()) + list(sums.values()) + list(sends.values()) + started:
         copy.wait_send()
 
 
-def exchange(n, name, ident, work, partial, ins, out_shapes, has_send, shape, tail=False, grads=()):
+def exchange(n, name, ident, work, partial, ins, out_shapes, has_send, shape, tail=False, grads=(), spread=()):
     parts, rows, width = shape
     has_sum = partial is not None
     relay = n == 4
     far = lax.axis_size("dp")
-    operands = ([partial] if has_sum else []) + list(ins) + list(grads)
+    operands = ([partial] if has_sum else []) + list(ins) + list(grads) + list(spread)
     shapes = ([jax.ShapeDtypeStruct((parts, n, rows, width), BF16)] if has_send else []) + [
         jax.ShapeDtypeStruct(s, t) for s, t in out_shapes
     ]
     shapes += [jax.ShapeDtypeStruct(g.shape[1:], F32) for g in grads]
+    shapes += [jax.ShapeDtypeStruct((2 * far,) + v.shape, v.dtype) for v in spread]
     sems = pltpu.SemaphoreType.DMA((parts, 4 if relay else n - 1))
     scratch = []
     if has_sum:
@@ -253,10 +277,12 @@
     for g in grads:
         scratch += [pltpu.VMEM((count,) + g.shape[1:], g.dtype) for count in (far, far - 1)]
         scratch += [pltpu.SemaphoreType.DMA((far,))] * 2 + [pltpu.SemaphoreType.DMA((far - 1,))] * 2
+    for _ in spread:
+        scratch += [pltpu.SemaphoreType.DMA((2 * far - 1,))] * 2
     return pl.pallas_call(
         functools.partial(
             exchange_kernel, n, far, parts, has_sum, has_send, tail, work, len(ins),
-            len(out_shapes), len(grads),
+            len(out_shapes), len(grads), len(spread),
         ),
         out_shape=shapes,
         in_specs=[VMEM_SPEC] * len(operands),
@@ -417,22 +443,23 @@
     hidden_here = w_up.shape[1]
     piece = (micro, own, width)
 
+    qkv_mine = jnp.concatenate([w_qkv[0], w_qkv[1], w_qkv[2]], 1)
+    qkv_weights = lax.all_gather(qkv_mine, share, axis=0, tiled=True)
     small = jnp.concatenate([v.reshape(-1) for v in (b_qv, b_up, ln_gains, ln_shifts)])
-    small = jnp.pad(small, (0, -small.size % (16 * 4 * cols))).reshape(-1, 4 * cols)
-    attn_mine = jnp.concatenate([w_qkv[0], w_qkv[1], w_qkv[2], w_out.T], 1)
-    attn_all = lax.all_gather(jnp.concatenate([attn_mine, small], 0), share, axis=0, tiled=False)
+    small = jnp.pad(small, (0, -small.size % (16 * 128))).reshape(16, -1)
     x_rows = inputs[:, 0]
-    (gathered,) = exchange(n, "gather_inputs", 0, work_inputs, None, [x_rows], [], True, piece)
+    gathered, small_all, out_all = exchange(
+        n, "gather_inputs", 0, work_inputs, None, [x_rows], [], True, piece,
+        spread=[small, w_out.T],
+    )
+    out_all = out_all.reshape(owners * depth, cols)
     gathered = gathered.reshape(micro * rows, width)
     up_all = lax.all_gather(w_up, share, axis=0, tiled=True)
     down_all = lax.all_gather(w_down.T, share, axis=0, tiled=True)
 
-    attn_weights = attn_all[:, :depth].reshape(owners * depth, 4 * cols)
-    q_weights = attn_weights[:, :cols]
-    kv_weights = attn_weights[:, cols : 3 * cols]
-    qkv_weights = attn_weights[:, : 3 * cols]
-    out_all = attn_weights[:, 3 * cols :]
-    small_all = attn_all[:, depth:].reshape(owners, -1)
+    q_weights = qkv_weights[:, :cols]
+    kv_weights = qkv_weights[:, cols:]
+    small_all = small_all.reshape(owners, -1)
     at = 0
     pieces = []
     for v in (b_qv, b_up, ln_gains, ln_shifts):
@@ -481,16 +508,19 @@
     g_up = owned(dot(normed_all, d_pre, TN))
     g_bup = jnp.sum(d_pre.astype(F32), 0).reshape(b_up.shape[0], owners, b_up.shape[1])
     g_bup = owned_small(jnp.swapaxes(g_bup, 0, 1).reshape(owners, -1))
-    d_attn, d_first, _, norm_sums, g_down, g_up, g_bup = exchange(
+    partial, g_down = lax.optimization_barrier((partial, g_down))
+    g_down = lax.psum_scatter(g_down, share, scatter_dimension=0, tiled=False)
+    d_attn, d_first, _, norm_sums, g_up, g_bup = exchange(
         n, "first_norm_back", 3, work_third, partial, [first, d_second, gains, sums_two],
         [(piece, F32), ((micro, 3, width), F32), ((6, width), F32)], True, piece, tail=True,
-        grads=[g_down, g_up, g_bup],
+        grads=[g_up, g_bup],
     )
 
     d_attn = d_attn.reshape(micro * rows, width)
     d_mixed = dot(d_attn, out_all, NN).astype(BF16).reshape(micro, rows, cols)
     norm_sums = jnp.swapaxes(norm_sums.reshape(6, owners, depth), 0, 1).reshape(owners, -1)
     g_out = owned(dot(d_attn, mixed_rows, TN))
+    d_mixed, g_down = lax.optimization_barrier((d_mixed, g_down))
     d_query, d_kv, d_far = attention_call(
         attend_back_kernel, "attend_back", queries, kv, kv_far, [d_mixed], [logs],
         ["row", "pair", "far"], 5, head,
@@ -522,7 +552,7 @@
         g_out.T,
         g_up,
         bup_grad,
-        g_down.T,
+        g_down.astype(F32).T,
         gain_grad,
         shift_grad,
     )

time: 327 us -> 314 us (0.960)
  Pallas kernels: 212 us -> 205 us
  waiting for transfers between devices: 12.4 us -> 7.91 us
    pallas_call x5, Pallas kernels: 186 us -> 178 us  [exchange(): pl.pallas_call(functools.partial(exchange_kernel, n, far, parts, has_sum,...]
    convert_element_type x3 -> x0, local copies, waits for them, and re-layouts: 5.44 us -> none  [the longest x1 2.36 us: local(): (dot(gathered, kv_weights, NN) + bias_kv).astype(BF16)]
    all_gather x1, waiting for transfers between devices: 11 us -> 6.49 us  [local(): qkv_weights = lax.all_gather(qkv_mine, share, axis=0, tiled=True)]
    optimization_barrier x0 -> x1, local copies, waits for them, and re-layouts: none -> 3.94 us  [local(): partial, g_down = lax.optimization_barrier((partial, g_down))]
    unnamed x77 -> x73, local copies, waits for them, and re-layouts: 16.4 us -> 17.8 us
  transfers between devices with their start and end apart: 5 -> 6, of which waited for: 1 -> 1; matrix products, arithmetic and copies ran while one was open for 10% -> 11% of each run, Pallas kernels for 22% -> 38%
where the time goes in v3:
time: 314 us; the launch traced here: 313 us
  Pallas kernels  205 us (65%)
  matrix products  54.1 us (17%)
  local copies, waits for them, and re-layouts  25.6 us (8%)
  between operations  14.2 us (5%)
  waiting for transfers between devices  7.91 us (3%)
  other arithmetic  5.63 us (2%)
    pallas_call x5, Pallas kernels, exchange(): pl.pallas_call(functools.partial(exchange_kernel, n, far, parts, has_sum,...  178 us
    dot_general x13, matrix products, dot(): lax.dot_general(left, right, (dims, ((), ())), preferred_element_type=F32)  54.1 us
    pallas_call x2, Pallas kernels, attention_call(): pl.pallas_call(functools.partial(kernel, head), grid=(micro, blocks), in_...  26.4 us
    unnamed x73, local copies, waits for them, and re-layouts  17.8 us
    all_gather x1, waiting for transfers between devices, local(): qkv_weights = lax.all_gather(qkv_mine, share, axis=0, tiled=True)  6.49 us
  transfers between devices with their start and end apart: 6, of which 1 were waited for; matrix products, arithmetic and copies ran while one was open for 11% of the time, Pallas kernels for 38%

profile of v3, /device:TPU:0, one launch (start us, length us, event | category | flops | bytes accessed | tf_op | source)
XLA Modules:
  0.0 312.9 jit_solution(7627071666043667206)
XLA Ops:
  7.2 0.9 slice_bitcast_fusion.2
  8.1 0.7 pad_maximum_fusion.1
  8.9 0.7 all-gather.6.cloned.1.call-update
  9.7 0.7 all-gather.8.cloned.1.call-update
  10.4 0.8 reshape.195
  11.2 0.8 copy.40
  12.0 0.9 copy.41
  13.0 0.8 fusion.17.refs_1_
  13.7 1.0 copy-done
  14.8 24.9 %gather_inputs.1 = (bf16[2,4,128,1024]{3,2,1,0:T(8,128)(2,1)S(1)}, bf16[8,16,128]{2,1,0:T(8,128)(2,1)S(1)}, bf16[8,128,256]{2,1,0:T(8,128)(2,1)S(1)}) custom-call(bf16[2,128,1024]{2,1,0:T(8,128)(2,1)S(1)} %bitcast.138, bf16[16,128]{1,0:T(8,128)(2,1)S(1)} %fusion.17.refs_1_, bf16[128,256]{1,0:T(8,128)(2,1)S(1)} %bitcast.152), custom_call_target="tpu_custom_call" | custom-call | flops 1000000 | bytes 60000000 | tf_op jit(solution)/shard_map/gather_inputs/pallas_call | solution.py:282
  39.7 1.4 copy-done.13
  41.3 6.5 %all-gather.4.cloned.1.call-done = bf16[1024,768]{1,0:T(8,128)(2,1)} async-done(((bf16[128,768]{1,0:T(8,128)(2,1)}), bf16[1024,768]{1,0:T(8,128)(2,1)}) %all-gather.4.cloned.1.call-update) | async-done | bytes 1572880 | tf_op jit(solution)/shard_map/all_gather | solution.py:447
  47.8 3.1 add_convert_fusion.1
  51.7 2.4 fusion.6
  54.2 11.1 %attend.1 = (bf16[2,512,256]{2,1,0:T(8,128)(2,1)S(1)}, f32[2,2,2,512]{3,2,1,0:T(2,128)S(1)}) custom-call(bf16[2,512,256]{2,1,0:T(8,128)(2,1)S(1)} %bitcast.176, bf16[2,512,512]{2,1,0:T(8,128)(2,1)S(1)} %bitcast.172, bf16[2,512,512]{2,1,0:T(8,128)(2,1)S(1)} %bitcast.173, bf16[2,512,512]{2,1,0:T(8,128)(2,1)} %collective-permute-done.k_far.v_far, ...), custom_call_target="tpu_custom_call" | custom-call | flops 4294967296 | bytes 20000000 | tf_op jit(solution)/shard_map/attend/pallas_call | solution.py:412
  65.3 2.1 convolution_convert_fusion.4
  67.4 38.8 %first_norm.1 = (bf16[2,4,128,1024]{3,2,1,0:T(8,128)(2,1)S(1)}, f32[2,128,1024]{2,1,0:T(8,128)S(1)}, bf16[2,128,1024]{2,1,0:T(8,128)(2,1)S(1)}) custom-call(bf16[2,4,128,1024]{3,2,1,0:T(8,128)(2,1)} %bitcast.179, bf16[2,128,1024]{2,1,0:T(8,128)(2,1)S(1)} %bitcast.139, f32[2,1024]{1,0:T(2,128)S(1)} %bitcast.155, f32[4,1024]{1,0:T(4,128)S(1)} %bitcast.153), custom_call_target="tpu_custom_call" | custom-call | flops 1000000 | bytes 60000000 | tf_op jit(solution)/shard_map/first_norm/pallas_call | solution.py:282
  106.2 1.3 copy-done.15
  107.5 7.4 %multiply_convert_fusion = (bf16[1024,1024]{1,0:T(8,128)(2,1)}, f32[1024,1024]{1,0:T(8,128)}) fusion(f32[1024]{0:T(1024)S(1)} %reshape.230, bf16[1024,1024]{1,0:T(8,128)(2,1)} %bitcast.167, bf16[1024,1024]{1,0:T(8,128)(2,1)} %all-gather.6.cloned.1.call-done), kind=kOutput, calls=%fused_computation.8 | convolution fusion | flops 2153775104 | bytes 10489856 | tf_op jit(solution)/shard_map/dot_general | solution.py:19
  114.9 5.9 %convolution_convert_fusion.3 = bf16[1024,1024]{1,0:T(8,128)(2,1)} fusion(bf16[1024,1024]{1,0:T(8,128)(2,1)} %get-tuple-element.111, bf16[1024,1024]{0,1:T(8,128)(2,1)} %all-gather.8.cloned.1.call-done), kind=kOutput, calls=%fused_computation.16 | convolution fusion | flops 2148532224 | bytes 6291456 | tf_op jit(solution)/shard_map/dot_general | solution.py:19
  120.8 38.6 %second_norm.1 = (bf16[2,4,128,1024]{3,2,1,0:T(8,128)(2,1)S(1)}, bf16[2,128,1024]{2,1,0:T(8,128)(2,1)S(1)}, f32[2,128,1024]{2,1,0:T(8,128)S(1)}, f32[2,3,1024]{2,1,0:T(4,128)S(1)}) custom-call(bf16[2,4,128,1024]{3,2,1,0:T(8,128)(2,1)} %bitcast.180, bf16[2,128,1024]{2,1,0:T(8,128)(2,1)S(1)} %get-tuple-element.43.refs_1_, bf16[2,128,1024]{2,1,0:T(8,128)(2,1)S(1)} %bitcast.147, ...), custom_call_target="tpu_custom_call" | custom-call | flops 1000000 | bytes 60000000 | tf_op jit(solution)/shard_map/second_norm/pallas_call | solution.py:282
  159.5 5.9 %convolution_convert_fusion.1 = bf16[1024,1024]{1,0:T(8,128)(2,1)} fusion(bf16[1024,1024]{1,0:T(8,128)(2,1)S(1)} %bitcast.169, bf16[1024,1024]{1,0:T(8,128)(2,1)} %get-tuple-element.111), kind=kOutput, calls=%fused_computation.14 | convolution fusion | flops 2148532224 | bytes 6291456 | tf_op jit(solution)/shard_map/dot_general | solution.py:19
  165.4 4.2 %convert_reduce_fusion = (f32[1024]{0:T(1024)S(1)}, bf16[1024,1024]{1,0:T(8,128)(2,1)S(1)}) fusion(f32[1024,1024]{1,0:T(8,128)S(1)} %copy-done.27, f32[1024]{0:T(1024)S(1)} %reshape.230, bf16[1024,1024]{1,0:T(8,128)(2,1)S(1)} %bitcast.170, bf16[1024,1024]{0,1:T(8,128)(2,1)S(1)} %copy-done.26), kind=kOutput, calls=%fused_computation.7 | convolution fusion | flops 2161114112 | bytes 10493952 | tf_op jit(solution)/shard_map/dot_general | solution.py:19
  169.6 3.7 %convolution_convert_fusion.2 = bf16[1024,1024]{1,0:T(8,128)(2,1)} fusion(bf16[1024,1024]{1,0:T(8,128)(2,1)S(1)} %get-tuple-element.114, bf16[1024,1024]{1,0:T(8,128)(2,1)S(1)} %copy-done.25), kind=kOutput, calls=%fused_computation.15 | convolution fusion | flops 2148532224 | bytes 6291456 | tf_op jit(solution)/shard_map/dot_general | solution.py:19
  173.3 3.9 %copy.45 = bf16[8,128,1024]{1,2,0:T(8,128)(2,1)} copy(bf16[8,128,1024]{2,1,0:T(8,128)(2,1)} %bitcast.184) | data formatting | bytes 4194304 | tf_op jit(solution)/shard_map/optimization_barrier | solution.py:511
  177.5 6.1 %convolution_convert_fusion = bf16[1024,1024]{1,0:T(8,128)(2,1)} fusion(bf16[1024,1024]{1,0:T(8,128)(2,1)} %bitcast.168, bf16[1024,1024]{1,0:T(8,128)(2,1)} %copy-done.28), kind=kOutput, calls=%fused_computation.13 | convolution fusion | flops 2148532224 | bytes 6291456 | tf_op jit(solution)/shard_map/dot_general | solution.py:19
  183.6 45.4 %first_norm_back.1 = (bf16[2,4,128,1024]{3,2,1,0:T(8,128)(2,1)}, f32[2,128,1024]{2,1,0:T(8,128)S(1)}, f32[2,3,1024]{2,1,0:T(4,128)}, f32[6,1024]{1,0:T(8,128)S(1...) custom-call(bf16[2,4,128,1024]{3,2,1,0:T(8,128)(2,1)} %bitcast.181, f32[2,128,1024]{2,1,0:T(8,128)S(1)} %get-tuple-element.47.refs_1_, ...), custom_call_target="tpu_custom_call" | custom-call | flops 1000000 | bytes 60000000 | tf_op jit(solution)/shard_map/first_norm_back/pallas_call | solution.py:282
  229.0 0.8 copy-done.7
  229.8 3.1 convolution_convert_fusion.8
  232.9 1.2 copy-done.17
  234.2 1.0 copy-done.19
  235.2 1.0 copy-done.20
  236.2 15.3 %attend_back.1 = (bf16[2,512,256]{2,1,0:T(8,128)(2,1)S(1)}, f32[2,2,512,256]{3,2,1,0:T(8,128)}, bf16[2,2,512,256]{3,2,1,0:T(8,128)(2,1)S(1)}) custom-call(bf16[2,512,256]{2,1,0:T(8,128)(2,1)S(1)} %bitcast.177, bf16[2,512,512]{2,1,0:T(8,128)(2,1)S(1)} %bitcast.174, bf16[2,512,512]{2,1,0:T(8,128)(2,1)S(1)} %bitcast.175, ...), custom_call_target="tpu_custom_call" | custom-call | flops 10737418240 | bytes 20000000 | tf_op jit(solution)/shard_map/attend_back/pallas_call | solution.py:412
  251.8 0.7 copy.52
  252.5 3.3 %convolution_convert_fusion.7 = bf16[1024,256]{1,0:T(8,128)(2,1)} fusion(bf16[1024,1024]{1,0:T(8,128)(2,1)} %bitcast.31, bf16[1024,256]{1,0:T(8,128)(2,1)S(1)} %bitcast.151), kind=kOutput, calls=%fused_computation.22 | convolution fusion | flops 537133056 | bytes 3145728 | tf_op jit(solution)/shard_map/dot_general | solution.py:19
  255.8 0.8 convert_bitcast_fusion
  256.6 1.6 add_convert_fusion
  258.3 1.9 copy-done.14
  260.2 1.9 convolution_convert_fusion.6
  262.8 5.0 %convolution_convert_fusion.5 = bf16[1024,1024]{1,0:T(8,128)(2,1)} fusion(bf16[1024,768]{1,0:T(8,128)(2,1)} %all-gather.4.cloned.1.call-done, bf16[1024,256]{1,0:T(8,128)(2,1)} %bitcast.190, bf16[1024,256]{1,0:T(8,128)(2,1)} %bitcast.187, bf16[1024,256]{1,0:T(8,128)(2,1)S(1)} %bitcast.143), kind=kOutput, calls=%fused_computation.18 | convolution fusion | flops 1616379904 | bytes 5242880 | tf_op jit(solution)/shard_map/dot_general | solution.py:19
  267.8 30.8 %input_grad.1 = (bf16[2,128,1024]{2,1,0:T(8,128)(2,1)S(1)}, f32[128,256]{1,0:T(8,128)S(1)}, f32[128,768]{1,0:T(8,128)S(1)}, f32[8,128]{1,0:T(8,128)S(1)}) custom-call(bf16[2,4,128,1024]{3,2,1,0:T(8,128)(2,1)} %bitcast.183, f32[2,128,1024]{2,1,0:T(8,128)S(1)} %get-tuple-element.57.refs_1_, bf16[8,128,256]{2,1,0:T(8,128)(2,1)S(1)} %bitcast.144, ...), custom_call_target="tpu_custom_call" | custom-call | flops 1000000 | bytes 60000000 | tf_op jit(solution)/shard_map/input_grad/pallas_call | solution.py:282
  298.6 0.6 copy-done.12
  299.5 0.6 slice.166
  300.0 1.7 copy.51
  301.9 0.9 copy.50
  303.9 0.8 copy.76
  304.7 0.8 copy.77
  305.5 0.8 copy.78
  (102 shorter events, 4.1 us)
Async XLA Ops:
  7.2 40.6 %all-gather.4.cloned.1.call-start = ((), (), s32[]{:S(2)}) async-start(), calls=%async_computation.1 | async-start | bytes 1769472 | tf_op jit(solution)/shard_map/all_gather | solution.py:447
  8.9 98.6 %all-gather.6.cloned.1.call-start = ((), (), s32[]{:S(2)}) async-start(), calls=%async_computation.2 | async-start | bytes 2359296 | tf_op jit(solution)/shard_map/all_gather | solution.py:457
  9.6 105.3 %all-gather.8.cloned.1.call-start = ((), (), s32[]{:S(2)}) async-start(), calls=%async_computation.3 | async-start | bytes 2359296 | tf_op jit(solution)/shard_map/all_gather | solution.py:458
  10.3 222.6 %reduce-scatter.2.cloned.1.call-start = ((), (), s32[]{:S(2)}) async-start(), calls=%async_computation.4 | async-start | bytes 2359296 | tf_op jit(solution)/shard_map/reduce_scatter | solution.py:512
  13.7 1.0 copy-start
  39.7 1.4 copy-start.13
  50.9 3.3 %copy-start.16 = (bf16[1024,512]{1,0:T(8,128)(2,1)}, bf16[1024,512]{1,0:T(8,128)(2,1)S(1)}, u32[]{:S(2)}) copy-start(bf16[1024,512]{1,0:T(8,128)(2,1)S(1)} %add_convert_fusion.1) | copy-start | bytes 3145732
  50.9 3.2 %collective-permute-start = (bf16[2,512,512]{2,1,0:T(8,128)(2,1)S(1)}, bf16[2,512,512]{2,1,0:T(8,128)(2,1)}, u32[]{:S(2)}, u32[]{:S(2)}) collective-permute-start(bf16[2,512,512]{2,1,0:T(8,128)(2,1)S(1)} %bitcast.171), channel_id=1, source_target_pairs={{0,4},{4,0},{1,5},{5,1},{2,6},{6,2},{3,7},{7,3},{8,12},{12,8},{9,1... | collective-permute-start | bytes 3145736 | tf_op jit(solution)/shard_map/ppermute | solution.py:475
  54.1 11.2 %copy-start.18 = (bf16[1024,256]{1,0:T(8,128)(2,1)}, bf16[1024,256]{1,0:T(8,128)(2,1)S(1)}, u32[]{:S(2)}) copy-start(bf16[1024,256]{1,0:T(8,128)(2,1)S(1)} %fusion.6) | copy-start | bytes 1572868
  65.3 2.1 copy-start.10
  65.3 2.1 copy-start.1
  106.2 1.3 copy-start.15
  114.9 5.9 %copy-start.9 = (bf16[2,1,128,1024]{3,2,1,0:T(8,128)(2,1)S(1)}, bf16[2,1,128,1024]{3,2,1,0:T(8,128)(2,1)}, u32[]{:S(2)}) copy-start(bf16[2,1,128,1024]{3,2,1,0:T(8,128)(2,1)} %param.19) | copy-start | bytes 1572868
  159.4 5.9 %copy-start.2 = (f32[2,128,1024]{2,1,0:T(8,128)}, f32[2,128,1024]{2,1,0:T(8,128)S(1)}, u32[]{:S(2)}) copy-start(f32[2,128,1024]{2,1,0:T(8,128)S(1)} %get-tuple-element.48.refs_2_) | copy-start | bytes 3145732
  159.4 5.9 %copy-start.5 = (bf16[2,128,1024]{2,1,0:T(8,128)(2,1)}, bf16[2,128,1024]{2,1,0:T(8,128)(2,1)S(1)}, u32[]{:S(2)}) copy-start(bf16[2,128,1024]{2,1,0:T(8,128)(2,1)S(1)} %get-tuple-element.44) | copy-start | bytes 1572868
  159.5 5.9 %copy-start.26 = (bf16[1024,1024]{0,1:T(8,128)(2,1)S(1)}, bf16[1024,1024]{0,1:T(8,128)(2,1)}, u32[]{:S(2)}) copy-start(bf16[1024,1024]{0,1:T(8,128)(2,1)} %all-gather.8.cloned.1.call-done) | copy-start | bytes 6291460
  159.5 5.9 %copy-start.27 = (f32[1024,1024]{1,0:T(8,128)S(1)}, f32[1024,1024]{1,0:T(8,128)}, u32[]{:S(2)}) copy-start(f32[1024,1024]{1,0:T(8,128)} %get-tuple-element.112) | copy-start | bytes 12582916
  165.4 4.2 %copy-start.25 = (bf16[1024,1024]{1,0:T(8,128)(2,1)S(1)}, bf16[1024,1024]{1,0:T(8,128)(2,1)}, u32[]{:S(2)}) copy-start(bf16[1024,1024]{1,0:T(8,128)(2,1)} %all-gather.6.cloned.1.call-done) | copy-start | bytes 6291460
  169.6 3.7 %copy-start.28 = (bf16[1024,1024]{1,0:T(8,128)(2,1)}, bf16[1024,1024]{1,0:T(8,128)(2,1)S(1)}, u32[]{:S(2)}) copy-start(bf16[1024,1024]{1,0:T(8,128)(2,1)S(1)} %get-tuple-element.114) | copy-start | bytes 6291460
  177.5 6.1 %copy-start.3 = (f32[2,128,1024]{2,1,0:T(8,128)S(1)}, f32[2,128,1024]{2,1,0:T(8,128)}, u32[]{:S(2)}) copy-start(f32[2,128,1024]{2,1,0:T(8,128)} %copy-done.2) | copy-start | bytes 3145732
  229.0 0.8 copy-start.7
  232.9 1.2 copy-start.17
  234.2 1.0 copy-start.19
  235.2 1.0 copy-start.20
  236.2 16.2 %copy-start.11 = (bf16[2,512,256]{2,1,0:T(8,128)(2,1)S(1)}, bf16[2,512,256]{2,1,0:T(8,128)(2,1)}, u32[]{:S(2)}) copy-start(bf16[2,512,256]{2,1,0:T(8,128)(2,1)} %copy-done.10) | copy-start | bytes 1572868
  251.6 5.1 %collective-permute-start.1 = (bf16[2,2,512,256]{3,2,1,0:T(8,128)(2,1)S(1)}, bf16[2,2,512,256]{3,2,1,0:T(8,128)(2,1)}, u32[]{:S(2)}, u32[]{:S(2)}) collective-permute-start(bf16[2,2,512,256]{3,2,1,0:T(8,128)(2,1)S(1)} %get-tuple-element.56), channel_id=1, source_target_pairs={{0,4},{4,0},{1,5},{5,1},{2,6},{6,2},{3,7},{7,3},{8,12},{12,8},{9,1... | collective-permute-start | bytes 3145736 | tf_op jit(solution)/shard_map/ppermute | solution.py:528
  252.5 3.3 %copy-start.24 = (bf16[1,128,1024]{1,2,0:T(8,128)(2,1)S(1)}, bf16[1,128,1024]{1,2,0:T(8,128)(2,1)}, u32[]{:S(2)}) copy-start(bf16[1,128,1024]{1,2,0:T(8,128)(2,1)} %reduce-scatter.2.cloned.1.call-done) | copy-start | bytes 786436
  252.5 4.2 %copy-start.21 = (f32[2,2,512,256]{3,2,1,0:T(8,128)S(1)}, f32[2,2,512,256]{3,2,1,0:T(8,128)}, u32[]{:S(2)}) copy-start(f32[2,2,512,256]{3,2,1,0:T(8,128)} %get-tuple-element.55) | copy-start | bytes 6291460
  258.2 2.0 copy-start.14
  258.3 3.8 %copy-start.22 = (bf16[1,2,512,256]{3,2,1,0:T(8,128)(2,1)}, bf16[1,2,512,256]{3,2,1,0:T(8,128)(2,1)S(1)}, u32[]{:S(2)}) copy-start(bf16[1,2,512,256]{3,2,1,0:T(8,128)(2,1)S(1)} %get-tuple-element.96) | copy-start | bytes 1572868
  258.3 3.8 %copy-start.23 = (bf16[1,2,512,256]{3,2,1,0:T(8,128)(2,1)}, bf16[1,2,512,256]{3,2,1,0:T(8,128)(2,1)S(1)}, u32[]{:S(2)}) copy-start(bf16[1,2,512,256]{3,2,1,0:T(8,128)(2,1)S(1)} %get-tuple-element.97) | copy-start | bytes 1572868
  262.8 5.0 %copy-start.4 = (bf16[1024,256]{1,0:T(8,128)(2,1)S(1)}, bf16[1024,256]{1,0:T(8,128)(2,1)}, u32[]{:S(2)}) copy-start(bf16[1024,256]{1,0:T(8,128)(2,1)} %convolution_convert_fusion.7) | copy-start | bytes 1572868
  298.6 0.7 copy-start.12
  299.2 4.7 %copy-start.6 = (bf16[2,128,1024]{2,1,0:T(8,128)(2,1)S(1)}, bf16[2,128,1024]{2,1,0:T(8,128)(2,1)}, u32[]{:S(2)}) copy-start(bf16[2,128,1024]{2,1,0:T(8,128)(2,1)} %copy-done.5) | copy-start | bytes 1572868
  299.3 6.3 %copy-start.8 = (f32[128,1024]{1,0:T(8,128)S(1)}, f32[128,1024]{1,0:T(8,128)}, u32[]{:S(2)}) copy-start(f32[128,1024]{1,0:T(8,128)} %copy-done.7) | copy-start | bytes 1572868
Sparse Core Ops, SparseCore 0:
  10.2 37.5 all-gather.3
  49.4 29.0 all-gather.5
  80.1 30.3 all-gather.7
  177.4 46.6 reduce-scatter.1

commit v4 on v3

--- a/solution.py
+++ b/solution.py
@@ -87,25 +87,22 @@
     place = lax.axis_index("dp")
     ahead = [lax.rem(place + j, far) for j in range(far)]
     owners = []
-    if n_grad:
+    if n_grad or n_spread:
         owners = [{"seq": 1 - side}] + [{"dp": ahead[j]} for j in range(1, far)]
-    if n_spread:
-        owners = [
-            {"dp": ahead[j], "seq": 1 - side if c else side}
-            for j in range(far)
-            for c in (0, 1)
-            if j or c
-        ]
     for target in owners:
         pl.semaphore_signal(barrier, inc=1, device_id=target, device_id_type=MESH)
     pl.semaphore_wait(barrier, n - 1 + len(owners))
 
-    spread_copies = []
+    spread_copies = {}
     mine = 2 * place + side
-    for src, dst, sems in zip(spread, spread_outs, spread_sems):
-        for at, target in enumerate(owners):
-            spread_copies.append(
-                start_at(src.at[...], dst.at[mine], sems[0].at[at], sems[1].at[at], target)
+    for at, (src, dst, sems) in enumerate(zip(spread, spread_outs, spread_sems)):
+        for j in range(far):
+            spread_copies[at, j] = start_at(
+                src.at[...],
+                dst.at[mine],
+                sems[0].at[j],
+                sems[1].at[j],
+                {"dp": ahead[j]} if j else {"seq": 1 - side},
             )
         dst[mine] = src[...]
 
@@ -245,8 +242,21 @@
             far_copies[at, j].wait_recv()
             total = total + scratch[1][j - 1].astype(F32)
         grad_outs[at][...] = total
-    for copy in spread_copies:
-        copy.wait()
+    for at, (dst, sems) in enumerate(zip(spread_outs, spread_sems)):
+        for j in range(1, far):
+            spread_copies[at, j].wait_recv()
+            slot = 2 * lax.rem(place + far - j, far) + side
+            spread_copies[at, far + j] = start_at(
+                dst.at[slot],
+                dst.at[slot],
+                sems[0].at[far - 1 + j],
+                sems[1].at[far - 1 + j],
+                {"seq": 1 - side},
+            )
+    for (_, j), copy in spread_copies.items():
+        if j == 0 or j >= far:
+            copy.wait_recv()
+    started += list(spread_copies.values())
     started += list(core_copies.values()) + list(far_copies.values())
     for copy in list(relays.values()) + list(sums.values()) + list(sends.values()) + started:
         copy.wait_send()
@@ -444,15 +454,15 @@
     piece = (micro, own, width)
 
     qkv_mine = jnp.concatenate([w_qkv[0], w_qkv[1], w_qkv[2]], 1)
-    qkv_weights = lax.all_gather(qkv_mine, share, axis=0, tiled=True)
     small = jnp.concatenate([v.reshape(-1) for v in (b_qv, b_up, ln_gains, ln_shifts)])
     small = jnp.pad(small, (0, -small.size % (16 * 128))).reshape(16, -1)
     x_rows = inputs[:, 0]
-    gathered, small_all, out_all = exchange(
+    gathered, small_all, out_all, qkv_weights = exchange(
         n, "gather_inputs", 0, work_inputs, None, [x_rows], [], True, piece,
-        spread=[small, w_out.T],
+        spread=[small, w_out.T, qkv_mine],
     )
     out_all = out_all.reshape(owners * depth, cols)
+    qkv_weights = qkv_weights.reshape(owners * depth, 3 * cols)
     gathered = gathered.reshape(micro * rows, width)
     up_all = lax.all_gather(w_up, share, axis=0, tiled=True)
     down_all = lax.all_gather(w_down.T, share, axis=0, tiled=True)
@@ -508,19 +518,19 @@
     g_up = owned(dot(normed_all, d_pre, TN))
     g_bup = jnp.sum(d_pre.astype(F32), 0).reshape(b_up.shape[0], owners, b_up.shape[1])
     g_bup = owned_small(jnp.swapaxes(g_bup, 0, 1).reshape(owners, -1))
-    partial, g_down = lax.optimization_barrier((partial, g_down))
-    g_down = lax.psum_scatter(g_down, share, scatter_dimension=0, tiled=False)
-    d_attn, d_first, _, norm_sums, g_up, g_bup = exchange(
+    partial, g_up = lax.optimization_barrier((partial, g_up))
+    g_up = lax.psum_scatter(g_up, share, scatter_dimension=0, tiled=False)
+    d_attn, d_first, _, norm_sums, g_down, g_bup = exchange(
         n, "first_norm_back", 3, work_third, partial, [first, d_second, gains, sums_two],
         [(piece, F32), ((micro, 3, width), F32), ((6, width), F32)], True, piece, tail=True,
-        grads=[g_up, g_bup],
+        grads=[g_down, g_bup],
     )
 
     d_attn = d_attn.reshape(micro * rows, width)
     d_mixed = dot(d_attn, out_all, NN).astype(BF16).reshape(micro, rows, cols)
     norm_sums = jnp.swapaxes(norm_sums.reshape(6, owners, depth), 0, 1).reshape(owners, -1)
     g_out = owned(dot(d_attn, mixed_rows, TN))
-    d_mixed, g_down = lax.optimization_barrier((d_mixed, g_down))
+    d_mixed, g_up = lax.optimization_barrier((d_mixed, g_up))
     d_query, d_kv, d_far = attention_call(
         attend_back_kernel, "attend_back", queries, kv, kv_far, [d_mixed], [logs],
         ["row", "pair", "far"], 5, head,
@@ -550,9 +560,9 @@
         qkv_grad,
         bqv_grad,
         g_out.T,
-        g_up,
+        g_up.astype(F32),
         bup_grad,
-        g_down.astype(F32).T,
+        g_down.T,
         gain_grad,
         shift_grad,
     )

time: 314 us -> 319 us (1.016)
  Pallas kernels: 205 us -> 227 us
  waiting for transfers between devices: 7.91 us -> 1.71 us
  matrix products: 54.1 us -> 48.2 us
  local copies, waits for them, and re-layouts: 25.6 us -> 21.3 us
    pallas_call x5, Pallas kernels: 178 us -> 201 us  [exchange(): pl.pallas_call(functools.partial(exchange_kernel, n, far, parts, has_sum,...]
    all_gather x1 -> x0, waiting for transfers between devices: 6.49 us -> none  [local(): qkv_weights = lax.all_gather(qkv_mine, share, axis=0, tiled=True)]
    dot_general x13, matrix products: 54.1 us -> 48.2 us  [dot(): lax.dot_general(left, right, (dims, ((), ())), preferred_element_type=F32)]
    optimization_barrier x1 -> x0, local copies, waits for them, and re-layouts: 3.94 us -> none  [local(): partial, g_down = lax.optimization_barrier((partial, g_down))]
    unnamed x73 -> x75, local copies, waits for them, and re-layouts: 17.8 us -> 17.5 us
  transfers between devices with their start and end apart: 6 -> 5, of which waited for: 1 -> 1; matrix products, arithmetic and copies ran while one was open for 11% -> 10% of each run, Pallas kernels for 38% -> 44%
where the time goes in v4:
time: 319 us
  Pallas kernels  227 us (71%)
  matrix products  48.2 us (15%)
  local copies, waits for them, and re-layouts  21.3 us (7%)
  between operations  14.2 us (4%)
  other arithmetic  5.12 us (2%)
    pallas_call x5, Pallas kernels, exchange(): pl.pallas_call(functools.partial(exchange_kernel, n, far, parts, has_sum,...  201 us
    dot_general x13, matrix products, dot(): lax.dot_general(left, right, (dims, ((), ())), preferred_element_type=F32)  48.2 us
    pallas_call x2, Pallas kernels, attention_call(): pl.pallas_call(functools.partial(kernel, head), grid=(micro, blocks), in_...  26.3 us
    unnamed x75, local copies, waits for them, and re-layouts  17.5 us
  transfers between devices with their start and end apart: 5, of which 1 were waited for; matrix products, arithmetic and copies ran while one was open for 10% of the time, Pallas kernels for 44%

profile of v4, /device:TPU:0, one launch (start us, length us, event | category | flops | bytes accessed | tf_op | source)
XLA Modules:
  0.0 318.7 jit_solution(3641958012863306493)
XLA Ops:
  7.2 0.7 all-gather.3.cloned.1.call-update
  8.0 0.7 all-gather.5.cloned.1.call-update
  8.7 0.8 reshape.198
  9.5 0.8 copy.40
  10.3 0.8 fusion.17.refs_1_
  11.1 0.9 copy.41
  12.0 0.9 slice_bitcast_fusion.2
  13.0 1.0 copy-done
  14.0 44.2 %gather_inputs.1 = (bf16[2,4,128,1024]{3,2,1,0:T(8,128)(2,1)S(1)}, bf16[8,16,128]{2,1,0:T(8,128)(2,1)S(1)}, bf16[8,128,256]{2,1,0:T(8,128)(2,1)S(1)}, bf16[8,128,768]{2,1,0:T(8,128)(2,1)S(1)}) custom-call(bf16[2,128,1024]{2,1,0:T(8,128)(2,1)S(1)} %bitcast.138, bf16[16,128]{1,0:T(8,128)(2,1)S(1)} %fusion.17.refs_1_, bf16[128,256]{1,0:T(8,128)(2,1)S(1)} %bitcast.153, ...), custom_call_target="tpu_custom_call" | custom-call | flops 1000000 | bytes 60000000 | tf_op jit(solution)/shard_map/gather_inputs/pallas_call | solution.py:292
  58.2 1.2 copy-done.20
  59.7 4.0 %add_convert_fusion.1 = bf16[1024,512]{1,0:T(8,128)(2,1)} fusion(bf16[1024,1024]{1,0:T(8,128)(2,1)S(1)} %bitcast.165, bf16[1024,768]{1,0:T(8,128)(2,1)} %bitcast.174, f32[512]{0:T(512)S(1)} %concatenate.24), kind=kOutput, calls=%fused_computation.12 | convolution fusion | flops 1074790400 | bytes 4196352 | tf_op jit(solution)/shard_map/dot_general | solution.py:19
  64.6 1.8 fusion.6
  66.7 10.9 %attend.1 = (bf16[2,512,256]{2,1,0:T(8,128)(2,1)S(1)}, f32[2,2,2,512]{3,2,1,0:T(2,128)S(1)}) custom-call(bf16[2,512,256]{2,1,0:T(8,128)(2,1)S(1)} %bitcast.177, bf16[2,512,512]{2,1,0:T(8,128)(2,1)} %bitcast.12.k_ref.v_ref, bf16[2,512,512]{2,1,0:T(8,128)(2,1)} %bitcast.12.k_ref.v_ref, bf16[2,512,512]{2,1,0:T(8,128)(2,1)} %collective-permute-done.k_far.v_far, ...), custom_call_target="tpu_custom_call" | custom-call | flops 4294967296 | bytes 20000000 | tf_op jit(solution)/shard_map/attend/pallas_call | solution.py:422
  77.6 0.8 copy-done.22
  78.4 2.1 convolution_convert_fusion.4
  80.5 38.7 %first_norm.1 = (bf16[2,4,128,1024]{3,2,1,0:T(8,128)(2,1)S(1)}, f32[2,128,1024]{2,1,0:T(8,128)S(1)}, bf16[2,128,1024]{2,1,0:T(8,128)(2,1)S(1)}) custom-call(bf16[2,4,128,1024]{3,2,1,0:T(8,128)(2,1)} %bitcast.180, bf16[2,128,1024]{2,1,0:T(8,128)(2,1)S(1)} %bitcast.139, f32[2,1024]{1,0:T(2,128)S(1)} %bitcast.156, f32[4,1024]{1,0:T(4,128)S(1)} %bitcast.154), custom_call_target="tpu_custom_call" | custom-call | flops 1000000 | bytes 60000000 | tf_op jit(solution)/shard_map/first_norm/pallas_call | solution.py:292
  119.2 1.3 copy-done.18
  120.5 7.4 %multiply_convert_fusion = (bf16[1024,1024]{1,0:T(8,128)(2,1)}, f32[1024,1024]{1,0:T(8,128)}) fusion(f32[1024]{0:T(1024)S(1)} %reshape.234, bf16[1024,1024]{1,0:T(8,128)(2,1)} %bitcast.172, bf16[1024,1024]{1,0:T(8,128)(2,1)} %all-gather.3.cloned.1.call-done), kind=kOutput, calls=%fused_computation.8 | convolution fusion | flops 2153775104 | bytes 10489856 | tf_op jit(solution)/shard_map/dot_general | solution.py:19
  127.9 6.0 %convolution_convert_fusion.3 = bf16[1024,1024]{1,0:T(8,128)(2,1)} fusion(bf16[1024,1024]{1,0:T(8,128)(2,1)} %get-tuple-element.113, bf16[1024,1024]{0,1:T(8,128)(2,1)} %all-gather.5.cloned.1.call-done), kind=kOutput, calls=%fused_computation.16 | convolution fusion | flops 2148532224 | bytes 6291456 | tf_op jit(solution)/shard_map/dot_general | solution.py:19
  133.9 38.9 %second_norm.1 = (bf16[2,4,128,1024]{3,2,1,0:T(8,128)(2,1)S(1)}, bf16[2,128,1024]{2,1,0:T(8,128)(2,1)S(1)}, f32[2,128,1024]{2,1,0:T(8,128)S(1)}, f32[2,3,1024]{2,1,0:T(4,128)S(1)}) custom-call(bf16[2,4,128,1024]{3,2,1,0:T(8,128)(2,1)} %bitcast.181, bf16[2,128,1024]{2,1,0:T(8,128)(2,1)S(1)} %get-tuple-element.45.refs_1_, bf16[2,128,1024]{2,1,0:T(8,128)(2,1)S(1)} %bitcast.148, ...), custom_call_target="tpu_custom_call" | custom-call | flops 1000000 | bytes 60000000 | tf_op jit(solution)/shard_map/second_norm/pallas_call | solution.py:292
  172.9 4.2 %convert_reduce_fusion = (f32[1024]{0:T(1024)S(1)}, bf16[1024,1024]{1,0:T(8,128)(2,1)S(1)}) fusion(f32[1024,1024]{1,0:T(8,128)S(1)} %copy-done.29, f32[1024]{0:T(1024)S(1)} %reshape.234, bf16[1024,1024]{1,0:T(8,128)(2,1)S(1)} %bitcast.170, bf16[1024,1024]{0,1:T(8,128)(2,1)S(1)} %copy-done.28), kind=kOutput, calls=%fused_computation.7 | convolution fusion | flops 2161114112 | bytes 10493952 | tf_op jit(solution)/shard_map/dot_general | solution.py:19
  177.1 3.8 %convolution_convert_fusion.1 = bf16[1024,1024]{1,0:T(8,128)(2,1)} fusion(bf16[1024,1024]{1,0:T(8,128)(2,1)S(1)} %bitcast.173, bf16[1024,1024]{1,0:T(8,128)(2,1)S(1)} %get-tuple-element.116), kind=kOutput, calls=%fused_computation.14 | convolution fusion | flops 2148532224 | bytes 6291456 | tf_op jit(solution)/shard_map/dot_general | solution.py:19
  180.9 3.8 %convolution_convert_fusion.2 = bf16[1024,1024]{1,0:T(8,128)(2,1)} fusion(bf16[1024,1024]{1,0:T(8,128)(2,1)S(1)} %get-tuple-element.116, bf16[1024,1024]{1,0:T(8,128)(2,1)S(1)} %copy-done.27), kind=kOutput, calls=%fused_computation.15 | convolution fusion | flops 2148532224 | bytes 6291456 | tf_op jit(solution)/shard_map/dot_general | solution.py:19
  185.0 6.1 %convolution_convert_fusion = bf16[1024,1024]{1,0:T(8,128)(2,1)} fusion(bf16[1024,1024]{1,0:T(8,128)(2,1)} %bitcast.171, bf16[1024,1024]{1,0:T(8,128)(2,1)} %get-tuple-element.113), kind=kOutput, calls=%fused_computation.13 | convolution fusion | flops 2148532224 | bytes 6291456 | tf_op jit(solution)/shard_map/dot_general | solution.py:19
  191.0 47.6 %first_norm_back.1 = (bf16[2,4,128,1024]{3,2,1,0:T(8,128)(2,1)S(1)}, f32[2,128,1024]{2,1,0:T(8,128)S(1)}, f32[2,3,1024]{2,1,0:T(4,128)}, f32[6,1024]{1,0:T(8,128...) custom-call(bf16[2,4,128,1024]{3,2,1,0:T(8,128)(2,1)} %bitcast.183, f32[2,128,1024]{2,1,0:T(8,128)S(1)} %get-tuple-element.49.refs_1_, ...), custom_call_target="tpu_custom_call" | custom-call | flops 1000000 | bytes 60000000 | tf_op jit(solution)/shard_map/first_norm_back/pallas_call | solution.py:292
  238.7 1.3 copy-done.16
  240.0 1.5 convolution_convert_fusion.8
  241.5 1.0 copy-done.24
  242.6 15.4 %attend_back.1 = (bf16[2,512,256]{2,1,0:T(8,128)(2,1)S(1)}, f32[2,2,512,256]{3,2,1,0:T(8,128)}, bf16[2,2,512,256]{3,2,1,0:T(8,128)(2,1)}) custom-call(bf16[2,512,256]{2,1,0:T(8,128)(2,1)S(1)} %bitcast.178, bf16[2,512,512]{2,1,0:T(8,128)(2,1)} %bitcast.12.k_ref.v_ref, bf16[2,512,512]{2,1,0:T(8,128)(2,1)} %bitcast.12.k_ref.v_ref, ...), custom_call_target="tpu_custom_call" | custom-call | flops 10737418240 | bytes 20000000 | tf_op jit(solution)/shard_map/attend_back/pallas_call | solution.py:422
  257.9 0.8 copy-done.4
  259.0 0.7 copy.51
  259.7 1.0 copy.52
  260.7 2.5 convolution_convert_fusion.7
  263.2 0.8 convert_element_type.136
  264.1 1.7 add_convert_fusion
  266.0 0.9 copy-done.5
  266.9 1.9 convolution_convert_fusion.6
  269.1 3.2 convolution_convert_fusion.5
  272.7 31.7 %input_grad.1 = (bf16[2,128,1024]{2,1,0:T(8,128)(2,1)S(1)}, f32[128,256]{1,0:T(8,128)S(1)}, f32[128,768]{1,0:T(8,128)S(1)}, f32[8,128]{1,0:T(8,128)S(1)}) custom-call(bf16[2,4,128,1024]{3,2,1,0:T(8,128)(2,1)} %bitcast.184, f32[2,128,1024]{2,1,0:T(8,128)S(1)} %get-tuple-element.59.refs_1_, bf16[8,128,256]{2,1,0:T(8,128)(2,1)S(1)} %bitcast.141, ...), custom_call_target="tpu_custom_call" | custom-call | flops 1000000 | bytes 60000000 | tf_op jit(solution)/shard_map/input_grad/pallas_call | solution.py:292
  304.4 0.8 copy-done.8
  305.2 0.7 copy-done.13
  306.0 0.6 slice.166
  306.6 1.7 copy.50
  308.5 0.9 copy.49
  309.4 0.6 pad_maximum_fusion.3
  309.9 0.6 pad_maximum_fusion.2
  310.5 0.8 copy.75
  311.3 0.8 copy.76
  (100 shorter events, 3.4 us)
Async XLA Ops:
  7.2 113.3 %all-gather.3.cloned.1.call-start = ((), (), s32[]{:S(2)}) async-start(), calls=%async_computation.1 | async-start | bytes 2359296 | tf_op jit(solution)/shard_map/all_gather | solution.py:467
  7.9 120.0 %all-gather.5.cloned.1.call-start = ((), (), s32[]{:S(2)}) async-start(), calls=%async_computation.2 | async-start | bytes 2359296 | tf_op jit(solution)/shard_map/all_gather | solution.py:468
  8.7 232.9 %reduce-scatter.2.cloned.1.call-start = ((), (), s32[]{:S(2)}) async-start(), calls=%async_computation.3 | async-start | bytes 2359296 | tf_op jit(solution)/shard_map/reduce_scatter | solution.py:522
  13.0 1.0 copy-start
  58.2 1.2 copy-start.20
  59.4 5.2 %copy-start.14 = (bf16[2,4,128,1024]{3,2,1,0:T(8,128)(2,1)}, bf16[2,4,128,1024]{3,2,1,0:T(8,128)(2,1)S(1)}, u32[]{:S(2)}) copy-start(bf16[2,4,128,1024]{3,2,1,0:T(8,128)(2,1)S(1)} %get-tuple-element.39) | copy-start | bytes 6291460
  63.6 3.0 collective-permute-start
  77.6 0.8 copy-start.22
  78.4 2.1 copy-start.11
  78.4 2.1 copy-start.1
  119.2 1.3 copy-start.18
  127.9 6.0 %copy-start.10 = (bf16[2,1,128,1024]{3,2,1,0:T(8,128)(2,1)S(1)}, bf16[2,1,128,1024]{3,2,1,0:T(8,128)(2,1)}, u32[]{:S(2)}) copy-start(bf16[2,1,128,1024]{3,2,1,0:T(8,128)(2,1)} %param.19) | copy-start | bytes 1572868
  127.9 44.9 %copy-start.29 = (f32[1024,1024]{1,0:T(8,128)S(1)}, f32[1024,1024]{1,0:T(8,128)}, u32[]{:S(2)}) copy-start(f32[1024,1024]{1,0:T(8,128)} %get-tuple-element.114) | copy-start | bytes 12582916
  133.9 38.9 %copy-start.28 = (bf16[1024,1024]{0,1:T(8,128)(2,1)S(1)}, bf16[1024,1024]{0,1:T(8,128)(2,1)}, u32[]{:S(2)}) copy-start(bf16[1024,1024]{0,1:T(8,128)(2,1)} %all-gather.5.cloned.1.call-done) | copy-start | bytes 6291460
  172.8 4.2 %copy-start.2 = (f32[2,128,1024]{2,1,0:T(8,128)}, f32[2,128,1024]{2,1,0:T(8,128)S(1)}, u32[]{:S(2)}) copy-start(f32[2,128,1024]{2,1,0:T(8,128)S(1)} %get-tuple-element.50.refs_2_) | copy-start | bytes 3145732
  172.8 4.2 %copy-start.6 = (bf16[2,128,1024]{2,1,0:T(8,128)(2,1)}, bf16[2,128,1024]{2,1,0:T(8,128)(2,1)S(1)}, u32[]{:S(2)}) copy-start(bf16[2,128,1024]{2,1,0:T(8,128)(2,1)S(1)} %get-tuple-element.46) | copy-start | bytes 1572868
  172.8 4.2 %copy-start.17 = (bf16[2,4,128,1024]{3,2,1,0:T(8,128)(2,1)}, bf16[2,4,128,1024]{3,2,1,0:T(8,128)(2,1)S(1)}, u32[]{:S(2)}) copy-start(bf16[2,4,128,1024]{3,2,1,0:T(8,128)(2,1)S(1)} %get-tuple-element.47) | copy-start | bytes 6291460
  172.9 4.2 %copy-start.19 = (bf16[2,4,128,1024]{3,2,1,0:T(8,128)(2,1)S(1)}, bf16[2,4,128,1024]{3,2,1,0:T(8,128)(2,1)}, u32[]{:S(2)}) copy-start(bf16[2,4,128,1024]{3,2,1,0:T(8,128)(2,1)} %copy-done.18) | copy-start | bytes 6291460
  177.1 3.8 %copy-start.27 = (bf16[1024,1024]{1,0:T(8,128)(2,1)S(1)}, bf16[1024,1024]{1,0:T(8,128)(2,1)}, u32[]{:S(2)}) copy-start(bf16[1024,1024]{1,0:T(8,128)(2,1)} %all-gather.3.cloned.1.call-done) | copy-start | bytes 6291460
  185.0 6.1 %copy-start.3 = (f32[2,128,1024]{2,1,0:T(8,128)S(1)}, f32[2,128,1024]{2,1,0:T(8,128)}, u32[]{:S(2)}) copy-start(f32[2,128,1024]{2,1,0:T(8,128)} %copy-done.2) | copy-start | bytes 3145732
  238.7 1.3 copy-start.16
  240.0 1.5 copy-start.23
  241.5 1.0 copy-start.24
  242.6 18.1 %copy-start.12 = (bf16[2,512,256]{2,1,0:T(8,128)(2,1)S(1)}, bf16[2,512,256]{2,1,0:T(8,128)(2,1)}, u32[]{:S(2)}) copy-start(bf16[2,512,256]{2,1,0:T(8,128)(2,1)} %copy-done.11) | copy-start | bytes 1572868
  257.9 0.8 copy-start.4
  258.7 5.3 %collective-permute-start.1 = (bf16[2,2,512,256]{3,2,1,0:T(8,128)(2,1)}, bf16[2,2,512,256]{3,2,1,0:T(8,128)(2,1)}, u32[]{:S(2)}, u32[]{:S(2)}) collective-permute-start(bf16[2,2,512,256]{3,2,1,0:T(8,128)(2,1)} %get-tuple-element.58), channel_id=1, source_target_pairs={{0,4},{4,0},{1,5},{5,1},{2,6},{6,2},{3,7},{7,3},{8,12},{12,8},{9,1... | collective-permute-start | bytes 3145736 | tf_op jit(solution)/shard_map/ppermute | solution.py:538
  260.7 2.5 copy-start.26
  260.7 3.4 %copy-start.25 = (f32[2,2,512,256]{3,2,1,0:T(8,128)S(1)}, f32[2,2,512,256]{3,2,1,0:T(8,128)}, u32[]{:S(2)}) copy-start(f32[2,2,512,256]{3,2,1,0:T(8,128)} %get-tuple-element.57) | copy-start | bytes 6291460
  264.1 1.9 copy-start.15
  265.8 1.1 copy-start.5
  266.9 2.2 copy-start.21
  304.4 0.8 copy-start.8
  305.2 0.7 copy-start.13
  305.8 4.7 %copy-start.7 = (bf16[2,128,1024]{2,1,0:T(8,128)(2,1)S(1)}, bf16[2,128,1024]{2,1,0:T(8,128)(2,1)}, u32[]{:S(2)}) copy-start(bf16[2,128,1024]{2,1,0:T(8,128)(2,1)} %copy-done.6) | copy-start | bytes 1572868
  305.8 5.5 %copy-start.9 = (bf16[2,128,1024]{2,1,0:T(8,128)(2,1)S(1)}, bf16[2,128,1024]{2,1,0:T(8,128)(2,1)}, u32[]{:S(2)}) copy-start(bf16[2,128,1024]{2,1,0:T(8,128)(2,1)} %copy-done.8) | copy-start | bytes 1572868
Sparse Core Ops, SparseCore 0:
  9.6 50.6 all-gather.2
  61.9 30.7 all-gather.4
  184.9 50.4 reduce-scatter.1
